TPU v7x, 32 devices: a whole 2x2x4 slice. The times are simulated.
32 devices in a mesh: dp: 4 (over z), expert: 8 (over y, x, core).
Axes of the slice: x: 2, y: 2, z: 4, core: 2. Of those that a mesh axis runs over, the one named last changes fastest.
Arguments:
- tokens: bfloat16 [4096, 2048], P(('dp', 'expert')), may hold values from -6 to 6
- expert_ids: int32 [4096, 4], P(('dp', 'expert')), may hold values from 0 to 7, all different within a row; in each aligned block of 128 rows (0 to 127, 128 to 255, ...) at most 128 rows name the same one
- gates: bfloat16 [4096, 4], P(('dp', 'expert')), may hold values from 0.099609375 to 1
- w_gate: bfloat16 [8, 2048, 384], P('expert'), may hold values from -0.125 to 0.125
- w_up: bfloat16 [8, 2048, 384], P('expert'), may hold values from -0.125 to 0.125
- w_down: bfloat16 [8, 384, 2048], P('expert'), may hold values from -0.3125 to 0.3125
- cotangent: bfloat16 [4096, 2048], P(('dp', 'expert')), may hold values from -6 to 6
Outputs:
- mixed: bfloat16 [4096, 2048], P(('dp', 'expert'))
- grad_tokens: bfloat16 [4096, 2048], P(('dp', 'expert'))
- grad_gate: float32 [8, 2048, 384], P('expert', 'dp')
- grad_up: float32 [8, 2048, 384], P('expert', 'dp')
- grad_down: float32 [8, 384, 2048], P('expert', 'dp')
Inputs may be any that keep to these rules, and one draw needn't show every extreme that they name: `expert_ids`: each row names 4 different experts. In each aligned block of 128 rows (the rows of one device) no expert is named by more than 128 rows, a bound that some block reaches.
All inputs are finite; a program needn't handle non-finite values.
Results may differ from a plain program's by a relative error of at most 0.024.
Values may be sent and summed in bfloat16 or wider, within the bound.
No kernel may reach another device: no remote copies, remote signals or barrier semaphores. Data moves between devices by JAX's collectives and lax.ppermute only.
A program may use at most 128 MiB of HBM per device.

v0:
```python
import functools

import jax
import jax.numpy as jnp
from jax import lax
from jax.experimental import pallas as pl
from jax.experimental.pallas import tpu as pltpu
from jax.sharding import PartitionSpec as P

F32 = jnp.float32
BF16 = jnp.bfloat16
LANES = 128
CORE, NEAR, FAR = 1, 2, 4
MEDIUM = pltpu.CompilerParams(vmem_limit_bytes=24 * 1024 * 1024)
SMALL = pltpu.CompilerParams(vmem_limit_bytes=12 * 1024 * 1024)
VMEM = pl.BlockSpec(memory_space=pltpu.VMEM)
SMEM = pl.BlockSpec(memory_space=pltpu.SMEM)
NT = (((1,), (1,)), ((), ()))


def cost(flops, arrays):
    size = sum(a.size * a.dtype.itemsize for a in arrays)
    return pl.CostEstimate(flops=flops // 64, bytes_accessed=size // 64, transcendentals=0)


def own_gate(gate_rows, expert_num):
    lane = lax.broadcasted_iota(jnp.int32, gate_rows.shape, 1)
    kept = jnp.where(lane == expert_num, gate_rows.astype(F32), 0.0)
    return jnp.sum(kept, axis=1, keepdims=True)


def pack_kernel(tok_ref, ids_ref, gates_ref, out_ref):
    rows, width = tok_ref.shape
    out_ref[:, :width] = tok_ref[...]
    lane = lax.broadcasted_iota(jnp.int32, (rows, LANES), 1)
    ids, gates = ids_ref[...], gates_ref[...].astype(F32)
    total = jnp.zeros((rows, LANES), F32)
    for k in range(ids.shape[1]):
        total = total + jnp.where(ids[:, k : k + 1] == lane, gates[:, k : k + 1], 0.0)
    out_ref[:, width:] = total.astype(BF16)


def packed(tokens, ids, gates):
    rows, width = tokens.shape
    return pl.pallas_call(
        pack_kernel,
        out_shape=jax.ShapeDtypeStruct((rows, width + LANES), BF16),
        compiler_params=SMALL,
    )(tokens, ids, gates)


def panels_kernel(wg_ref, wu_ref, wd_ref, wide_ref, down_ref):
    hid = wg_ref.shape[1]
    wide_ref[:, :hid] = wg_ref[...]
    wide_ref[:, hid:] = wu_ref[...]
    down_ref[...] = wd_ref[...]


def panels(wg, wu, wd):
    width, hid = wg.shape
    outs = (jax.ShapeDtypeStruct((width, 2 * hid), BF16), jax.ShapeDtypeStruct(wd.shape, BF16))
    return pl.pallas_call(
        panels_kernel,
        out_shape=outs,
        in_specs=[VMEM] * 3,
        out_specs=(VMEM, VMEM),
        compiler_params=SMALL,
        cost_estimate=cost(width, outs),
    )(wg, wu, wd)


def hidden_kernel(blocks, me_ref, *refs):
    toks, cots = refs[:blocks], refs[blocks : 2 * blocks]
    wide_ref, down_ref, act_ref, hid_ref, og_ref = refs[2 * blocks :]
    each, width = cots[0].shape
    hid = down_ref.shape[0]
    rows = jnp.concatenate([t[:, :width] for t in toks], axis=0)
    pre = jnp.dot(rows, wide_ref[...], preferred_element_type=F32)
    for i in range(blocks):
        gate_col = own_gate(toks[i][:, width:], me_ref[0])
        og_ref[i * each : (i + 1) * each, :] = (gate_col * cots[i][...].astype(F32)).astype(BF16)
    act_grad = lax.dot_general(og_ref[...], down_ref[...], NT, preferred_element_type=F32)
    pre_gate, pre_up = pre[:, :hid], pre[:, hid:]
    s = 1.0 / (1.0 + jnp.exp(-pre_gate))
    act_ref[...] = (pre_gate * s * pre_up).astype(BF16)
    hid_ref[:, :hid] = (act_grad * pre_up * s * (1.0 + pre_gate * (1.0 - s))).astype(BF16)
    hid_ref[:, hid:] = (act_grad * pre_gate * s).astype(BF16)


def hidden(me, toks, cots, wide, down):
    blocks = len(toks)
    rows = blocks * cots[0].shape[0]
    hid, width = down.shape
    outs = tuple(jax.ShapeDtypeStruct((rows, n), BF16) for n in (hid, 2 * hid, width))
    return pl.pallas_call(
        functools.partial(hidden_kernel, blocks),
        out_shape=outs,
        in_specs=[SMEM] + [VMEM] * (2 * blocks + 2),
        out_specs=(VMEM,) * 3,
        compiler_params=MEDIUM,
        cost_estimate=cost(6 * rows * width * hid, (*toks, *cots, wide, down) + outs),
    )(me, *toks, *cots, wide, down)


def rows_kernel(blocks, groups, part, places, more, me_ref, *refs):
    toks, refs = refs[:blocks], refs[blocks:]
    acts, hids, refs = refs[:groups], refs[groups : 2 * groups], refs[2 * groups :]
    wide_ref, down_ref = refs[:2]
    added, outs = refs[2 : 2 + more], refs[2 + more :]
    width = down_ref.shape[1]
    each = toks[0].shape[0]
    gate_col = own_gate(jnp.concatenate([t[:, width:] for t in toks], axis=0), me_ref[0])

    def joined(refs):
        size = refs[0].shape[0] // 2
        return jnp.concatenate([refs[0][part * size : (part + 1) * size, :]] + [r[...] for r in refs[1:]], axis=0)

    def put(values, number, columns):
        for i in range(blocks):
            piece = values[i * each : (i + 1) * each]
            if more:
                other = added[number][i * each : (i + 1) * each, columns]
                piece = (piece.astype(F32) + other.astype(F32)).astype(BF16)
            array, block = places[number][i]
            outs[array][block * each : (block + 1) * each, columns] = piece

    act, hidden_grads = joined(acts), joined(hids)
    step = width // 4
    for j in range(4):
        columns = slice(j * step, (j + 1) * step)
        expert_out = jnp.dot(act, down_ref[:, columns], preferred_element_type=F32)
        put((gate_col * expert_out).astype(BF16), 0, columns)
        grad = lax.dot_general(hidden_grads, wide_ref[columns, :], NT, preferred_element_type=F32)
        put(grad.astype(BF16), 1, columns)


def rows_out(me, toks, acts, hids, part, wide, down, added, places):
    blocks, groups = len(toks), len(acts)
    each = toks[0].shape[0]
    hid, width = down.shape
    flat = places[0] + places[1]
    sizes = [sum(array == k for array, _ in flat) for k in range(1 + max(array for array, _ in flat))]
    outs = tuple(jax.ShapeDtypeStruct((n * each, width), BF16) for n in sizes)
    return pl.pallas_call(
        functools.partial(rows_kernel, blocks, groups, part, places, len(added)),
        out_shape=outs,
        in_specs=[SMEM] + [VMEM] * (blocks + 2 * groups + 2 + len(added)),
        out_specs=(VMEM,) * len(outs),
        compiler_params=MEDIUM,
        cost_estimate=cost(6 * blocks * each * width * hid, (wide, down) + outs),
    )(me, *toks, *acts, *hids, wide, down, *added)


TN = (((0,), (0,)), ((), ()))


def wide_grad_kernel(blocks, groups, first, count, order_ref, *refs):
    toks, hids, start, outs = refs[:blocks], refs[blocks : blocks + groups], refs[blocks + groups : -count], refs[-count:]
    hidden_grads = jnp.concatenate([h[...] for h in hids], axis=0)
    tile = outs[0].shape[0]
    for k in range(count):
        at = pl.multiple_of(order_ref[first + k] * tile, tile)
        rows = jnp.concatenate([t[:, pl.ds(at, tile)] for t in toks], axis=0)
        total = lax.dot_general(rows, hidden_grads, TN, preferred_element_type=F32)
        if start:
            total = total + start[0][...]
        outs[k][...] = total.astype(outs[k].dtype)


def wide_grads(order, toks, hids, width, first, count, start=(), kind=BF16):
    blocks = len(toks)
    each = toks[0].shape[0]
    both, tile = hids[0].shape[1], width // 4
    out = jax.ShapeDtypeStruct((tile, both), kind)
    return pl.pallas_call(
        functools.partial(wide_grad_kernel, blocks, len(hids), first, count),
        out_shape=(out,) * count,
        in_specs=[SMEM] + [VMEM] * (blocks + len(hids) + len(start)),
        out_specs=(VMEM,) * count,
        compiler_params=MEDIUM,
        cost_estimate=cost(2 * count * blocks * each * both * tile, tuple(hids) + (out,) * count),
    )(order, *toks, *hids, *start)


def down_grad_kernel(groups, order_ref, *refs):
    acts, ogs, outs, full = refs[:groups], refs[groups : 2 * groups], refs[2 * groups : -1], refs[-1]
    act = jnp.concatenate([a[...] for a in acts], axis=0)
    step = full.shape[1]
    size = full.shape[0] // 4
    for j in range(4):
        columns = slice(j * step, (j + 1) * step)
        og = jnp.concatenate([o[:, columns] for o in ogs], axis=0)
        full[...] = lax.dot_general(act, og, TN, preferred_element_type=F32)
        for k in range(4):
            at = pl.multiple_of(order_ref[k] * size, size)
            outs[k][:, columns] = full[pl.ds(at, size), :].astype(BF16)


def down_grads(order, acts, ogs):
    hid = acts[0].shape[1]
    rows = sum(a.shape[0] for a in acts)
    width = ogs[0].shape[1]
    out = jax.ShapeDtypeStruct((hid // 4, width), BF16)
    return pl.pallas_call(
        functools.partial(down_grad_kernel, len(acts)),
        out_shape=(out,) * 4,
        in_specs=[SMEM] + [VMEM] * (2 * len(acts)),
        out_specs=(VMEM,) * 4,
        scratch_shapes=[pltpu.VMEM((hid, width // 4), F32)],
        compiler_params=MEDIUM,
        cost_estimate=cost(2 * rows * hid * width, tuple(acts) + tuple(ogs)),
    )(order, *acts, *ogs)


PIECE = 256


def pieces(wide_shape, down_shape):
    at = 0
    for number, (rows, columns) in enumerate((wide_shape, down_shape)):
        for j in range(columns // PIECE):
            yield number, slice(at, at + rows), slice(j * PIECE, (j + 1) * PIECE)
            at += rows


def join_kernel(order_ref, wide_own, down_own, *refs):
    came, out_ref = refs[:-1], refs[-1]
    owns = wide_own, down_own
    for number, rows, part in pieces(wide_own.shape, down_own.shape):
        own = owns[number][:, part]
        if came:
            other = came[0][rows, :] if len(came) == 1 else came[number][:, part]
            other = jnp.where(order_ref[4] == 1, other.astype(F32), 0.0)
            own = (own.astype(F32) + other).astype(BF16)
        out_ref[rows, :] = own


def join(order, wide_own, down_own, *came):
    out = jax.ShapeDtypeStruct(((wide_own.size + down_own.size) // PIECE, PIECE), BF16)
    return pl.pallas_call(
        join_kernel,
        out_shape=out,
        in_specs=[SMEM] + [VMEM] * (2 + len(came)),
        compiler_params=SMALL,
        cost_estimate=cost(wide_own.size, (out,)),
    )(order, wide_own, down_own, *came)


def base_kernel(order_ref, wide_own, down_own, wide_one, down_one, two_ref, wide_out, down_out):
    owns, ones, outs = (wide_own, down_own), (wide_one, down_one), (wide_out, down_out)
    for number, rows, part in pieces(wide_own.shape, down_own.shape):
        came = ones[number][:, part].astype(F32) + two_ref[rows, :].astype(F32)
        came = jnp.where(order_ref[4] == 1, 0.0, came)
        outs[number][:, part] = owns[number][:, part].astype(F32) + came


def base_terms(order, wide_own, down_own, wide_one, down_one, two):
    outs = tuple(jax.ShapeDtypeStruct(a.shape, F32) for a in (wide_own, down_own))
    return pl.pallas_call(
        base_kernel,
        out_shape=outs,
        in_specs=[SMEM] + [VMEM] * 5,
        compiler_params=SMALL,
        cost_estimate=cost(wide_own.size, outs),
    )(order, wide_own, down_own, wide_one, down_one, two)


def finish_kernel(wide_ref, down_ref, up_ref, low_ref, gate_out, up_out, down_out):
    bases, outs = (wide_ref, down_ref), ((gate_out, up_out), (down_out,))
    for number, rows, part in pieces(wide_ref.shape, down_ref.shape):
        came = up_ref[rows, :].astype(F32) + low_ref[rows, :].astype(F32)
        total = bases[number][:, part] + came
        for k, out in enumerate(outs[number]):
            size = out.shape[1]
            a, b = max(part.start, k * size), min(part.stop, (k + 1) * size)
            if a < b:
                out[:, a - k * size : b - k * size] = total[:, a - part.start : b - part.start]


def finish(wide, down, one, two):
    rows, both = wide.shape
    outs = (jax.ShapeDtypeStruct((rows, both // 2), F32),) * 2 + (jax.ShapeDtypeStruct(down.shape, F32),)
    return pl.pallas_call(
        finish_kernel,
        out_shape=outs,
        compiler_params=SMALL,
        cost_estimate=cost(wide.size, outs),
    )(wide, down, one, two)


def after(values, earlier):
    return lax.optimization_barrier((values, earlier))[0]


def pair_sums_kernel(places, *refs):
    for terms, out_ref in zip(places, refs[-2:]):
        each = out_ref.shape[0]
        values = [refs[k][block * each : (block + 1) * each, :].astype(F32) for k, block in terms]
        out_ref[...] = sum(values[1:], values[0]).astype(BF16)


def pair_sums(each, first, second):
    arrays = [a for a, _ in first + second]
    blocks = [block for _, block in first + second]
    numbered = tuple(enumerate(blocks))
    out = jax.ShapeDtypeStruct((each, arrays[0].shape[1]), BF16)
    return pl.pallas_call(
        functools.partial(pair_sums_kernel, (numbered[: len(first)], numbered[len(first) :])),
        out_shape=(out, out),
        in_specs=[VMEM] * len(arrays),
        out_specs=(VMEM, VMEM),
        compiler_params=SMALL,
        cost_estimate=cost(out.size, (out,)),
    )(*arrays)


LINE_ORDER = ((3, 2, 1, 0, 0), (0, 3, 2, 1, 1), (3, 0, 1, 2, 1), (0, 1, 2, 3, 0))


def per_device(tokens, expert_ids, gates, w_gate, w_up, w_down, cotangent):
    width = tokens.shape[1]
    group = lax.axis_size("expert")
    shards = lax.axis_size("dp")
    assert group == 8
    me = lax.axis_index("expert").astype(jnp.int32).reshape(1)
    z = lax.axis_index("dp")
    wg, wu, wd = w_gate[0], w_up[0], w_down[0]

    def flip(array, bit):
        return lax.ppermute(array, "expert", [(i, i ^ bit) for i in range(group)])

    line = shards == 4
    table = jnp.asarray(LINE_ORDER if line else ((0, 1, 2, 3, 0),), jnp.int32)
    order = table[z if line else 0]
    tokens = after(tokens, (order, me))
    cot_0 = cotangent
    tok_0 = packed(tokens, expert_ids, gates)
    tok_x, cot_y = flip(tok_0, NEAR), flip(cot_0, FAR)
    cot_x, tok_y = flip(cot_0, NEAR), flip(tok_0, FAR)
    cot_d, tok_d = flip(cot_y, NEAR), flip(tok_x, FAR)

    toks_a, cots_a = [tok_0, tok_x, tok_y], [cot_0, cot_x, cot_y]
    wide_panel, down_panel = panels(wg, wu, wd)
    cots_a += [flip(c, CORE) for c in [after(cot_0, wide_panel)] + cots_a[1:]]
    toks_a += [flip(t, CORE) for t in toks_a]
    act_a, hid_a, og_a = hidden(me, toks_a, cots_a, wide_panel, down_panel)
    tok_d, cot_d = after((tok_d, cot_d), act_a)
    tok_e, cot_e = flip(tok_d, CORE), flip(cot_d, CORE)
    act_d, hid_d, og_d = hidden(me, [tok_d], [cot_d], wide_panel, down_panel)
    toks = toks_a + [tok_d]
    (wide_part,) = wide_grads(order, toks, (hid_a, hid_d), width, 0, 1, kind=F32)
    tok_e, cot_e = after((tok_e, cot_e), wide_part)
    act_e, hid_e, og_e = hidden(me, [tok_e], [cot_e], wide_panel, down_panel)

    def move(array, pairs):
        return lax.ppermute(array, "dp", pairs) if line else array

    one_pairs = [(0, 1), (1, 0), (2, 3), (3, 2)]
    two_pairs = [(0, 1), (1, 3), (3, 2), (2, 0)]
    end_pairs, mid_pairs = [(0, 1), (3, 2)], [(1, 2), (2, 1)]
    toks = toks + [tok_e]
    wide_0 = wide_grads(order, [tok_e], (hid_e,), width, 0, 1, start=(wide_part,))
    wide_one = move(wide_0[0], one_pairs)
    act_a = after(act_a, wide_0)
    down = down_grads(order, (act_a, act_d, act_e), (og_a, og_d, og_e))
    down_one = move(down[0], one_pairs)
    hid_a = after(hid_a, down)
    wide = wide_0 + wide_grads(order, toks, (hid_a, hid_d, hid_e), width, 1, 3)
    act_a = after(act_a, wide[1])
    there = tuple((0, i) for i in range(4)), tuple((1, i) for i in range(4))
    sent = rows_out(me, toks_a[3:] + [tok_e], (act_a, act_e), (hid_a, hid_e), 1, wide_panel, down_panel, (), there)
    if line:
        wide_one, down_one = after((wide_one, down_one), sent)
        second = join(order, wide[1], down[1], wide_one, down_one)
        two = move(second, two_pairs)
        sent = after(sent, second)
    sent = [flip(a, CORE) for a in sent]
    here = ((0, 0), (2, 0), (1, 0), (2, 1)), ((3, 0), (4, 0), (5, 0), (5, 1))
    kept = rows_out(me, toks_a[:3] + [tok_d], (act_a, act_d), (hid_a, hid_d), 0, wide_panel, down_panel, sent, here)
    out_0, out_y, out_near, grad_0, grad_x, grad_far = kept
    out_near, grad_far = flip(out_near, NEAR), flip(grad_far, FAR)
    hid_size = wd.shape[0]
    each = tokens.shape[0]
    if line:
        own_last = join(order, *after((wide[2], down[2]), kept))
        two = after(two, own_last)
        last = join(order, wide[2], down[2], two)
        last_end, last_mid = move(own_last, end_pairs), move(last, mid_pairs)
        out_near, grad_far = after((out_near, grad_far), last)
    out_y, grad_x = pair_sums(each, [(out_y, 0), (out_near, 1)], [(grad_x, 0), (grad_far, 1)])
    out_yy, grad_xx = flip(out_y, FAR), flip(grad_x, NEAR)
    if line:
        base = base_terms(order, wide[3], down[3], wide_one, down_one, after(two, (out_y, grad_x)))
    mixed, grad_tokens = pair_sums(
        each, [(out_0, 0), (out_near, 0), (out_yy, 0)], [(grad_0, 0), (grad_far, 0), (grad_xx, 0)]
    )
    if line:
        base, mixed, grad_tokens = lax.optimization_barrier((base, mixed, grad_tokens))
        last_end, last_mid = after((last_end, last_mid), (mixed, grad_tokens))
        grad_gate, grad_up, grad_down = finish(*base, last_end, last_mid)
    else:
        wide_all = jnp.concatenate(wide, axis=0)
        grad_wide = lax.psum_scatter(wide_all, "dp", scatter_dimension=0, tiled=True).astype(F32)
        grad_gate, grad_up = grad_wide[:, :hid_size], grad_wide[:, hid_size:]
        grad_down = lax.psum_scatter(jnp.concatenate(down, axis=0), "dp", scatter_dimension=0, tiled=True).astype(F32)
    return (mixed, grad_tokens, grad_gate[None], grad_up[None], grad_down[None])


def solution(mesh):
    return jax.shard_map(
        per_device,
        mesh=mesh,
        in_specs=(
            P(("dp", "expert"), None),
            P(("dp", "expert"), None),
            P(("dp", "expert"), None),
            P("expert", None, None),
            P("expert", None, None),
            P("expert", None, None),
            P(("dp", "expert"), None),
        ),
        out_specs=(
            P(("dp", "expert"), None),
            P(("dp", "expert"), None),
            P("expert", "dp", None),
            P("expert", "dp", None),
            P("expert", "dp", None),
        ),
        check_vma=False,
    )
```

profile of v0, /device:TPU:10, one launch (start us, length us, event | category | flops | bytes accessed | tf_op | source)
XLA Modules:
  0.0 140.4 jit_solution(12233165986374770154)
XLA Ops:
  1.2 1.5 %collective-permute-start.6 = (bf16[128,2048]{1,0:T(8,128)(2,1)}, bf16[128,2048]{1,0:T(8,128)(2,1)S(1)}, u32[]{:S(2)}, u32[]{:S(2)}) collective-permute-start(bf16[128,2048]{1,0:T(8,128)(2,1)} %refs_6_.1), channel_id=1, source_target_pairs={{0,4},{1,5},{2,6},{3,7},{4,0},{5,1},{6,2},{7,3},{8,12},{9,13},{10,... | collective-permute-start | bytes 1572872 | tf_op jit(solution)/shard_map/ppermute | solution.py:330
  6.8 1.5 %collective-permute-start = (bf16[128,2176]{1,0:T(8,128)(2,1)S(1)}, bf16[128,2176]{1,0:T(8,128)(2,1)S(1)}, u32[]{:S(2)}, u32[]{:S(2)}) collective-permute-start(bf16[128,2176]{1,0:T(8,128)(2,1)S(1)} %shard_map.119.refs_0_), channel_id=1, source_target_pairs={{0,2},{1,3},{2,0},{3,1},{4,6},{5,7},{6,4},{7,5},{8,10},{9,11},{10,... | collective-permute-start | bytes 1671176 | tf_op jit(solution)/shard_map/ppermute | solution.py:330
  8.3 1.4 %copy-done = bf16[1,2048,384]{2,1,0:T(8,128)(2,1)S(1)} copy-done((bf16[1,2048,384]{2,1,0:T(8,128)(2,1)S(1)}, bf16[1,2048,384]{2,1,0:T(8,128)(2,1)}, u32[]{:S(2)}) %copy-start) | copy-done | bytes 1572888
  9.7 1.4 %copy-done.1 = bf16[1,2048,384]{2,1,0:T(8,128)(2,1)S(1)} copy-done((bf16[1,2048,384]{2,1,0:T(8,128)(2,1)S(1)}, bf16[1,2048,384]{2,1,0:T(8,128)(2,1)}, u32[]{:S(2)}) %copy-start.1) | copy-done | bytes 1572888
  11.1 1.4 %copy-done.2 = bf16[1,384,2048]{2,1,0:T(8,128)(2,1)S(1)} copy-done((bf16[1,384,2048]{2,1,0:T(8,128)(2,1)S(1)}, bf16[1,384,2048]{2,1,0:T(8,128)(2,1)}, u32[]{:S(2)}) %copy-start.2) | copy-done | bytes 1572888
  12.9 2.8 %collective-permute-done.8.refs_7_ = bf16[128,2048]{1,0:T(8,128)(2,1)S(1)} collective-permute-done((bf16[128,2048]{1,0:T(8,128)(2,1)}, bf16[128,2048]{1,0:T(8,128)(2,1)S(1)}, u32[]{:S(2)}, u32[]{:S(2)}) %collective-permute-start.8) | collective-permute-done | bytes 524320 | tf_op jit(solution)/shard_map/ppermute | solution.py:330
  16.3 10.5 %collective-permute-done.1.refs_2_ = bf16[128,2176]{1,0:T(8,128)(2,1)S(1)} collective-permute-done((bf16[128,2176]{1,0:T(8,128)(2,1)S(1)}, bf16[128,2176]{1,0:T(8,128)(2,1)S(1)}, u32[]{:S(2)}, u32[]{:S(2)}) %collective-permute-start.1) | collective-permute-done | bytes 557088 | tf_op jit(solution)/shard_map/ppermute | solution.py:330
  27.3 1.5 %collective-permute-start.5 = (bf16[128,2176]{1,0:T(8,128)(2,1)S(1)}, bf16[128,2176]{1,0:T(8,128)(2,1)S(1)}, u32[]{:S(2)}, u32[]{:S(2)}) collective-permute-start(bf16[128,2176]{1,0:T(8,128)(2,1)S(1)} %collective-permute-done.refs_1_), channel_id=1, source_target_pairs={{0,4},{1,5},{2,6},{3,7},{4,0},{5,1},{6,2},{7,3},{8,12},{9,13},{10,... | collective-permute-start | bytes 1671176 | tf_op jit(solution)/shard_map/ppermute | solution.py:330
  28.8 1.6 %collective-permute-start.7 = (bf16[128,2048]{1,0:T(8,128)(2,1)S(1)}, bf16[128,2048]{1,0:T(8,128)(2,1)S(1)}, u32[]{:S(2)}, u32[]{:S(2)}) collective-permute-start(bf16[128,2048]{1,0:T(8,128)(2,1)S(1)} %collective-permute-done.6.refs_8_), channel_id=1, source_target_pairs={{0,2},{1,3},{2,0},{3,1},{4,6},{5,7},{6,4},{7,5},{8,10},{9,11},{10,... | collective-permute-start | bytes 1572872 | tf_op jit(solution)/shard_map/ppermute | solution.py:330
  30.7 4.5 %shard_map.121 = (bf16[768,384]{1,0:T(8,128)(2,1)S(1)}, bf16[768,768]{1,0:T(8,128)(2,1)S(1)}, bf16[768,2048]{1,0:T(8,128)(2,1)S(1)}) custom-call(s32[1]{0:T(128)} %bitcast.1.me_ref, bf16[128,2176]{1,0:T(8,128)(2,1)S(1)} %shard_map.119.refs_0_, bf16[128,2176]{1,0:T(8,128)(2,1)S(1)} %collective-permute-done.refs_1_, ...), custom_call_target="tpu_custom_call" | custom-call | flops 56623104 | bytes 251904 | tf_op jit(solution)/shard_map/pallas_call | solution.py:95
  35.2 7.9 %collective-permute-done.7.refs_1_ = bf16[128,2048]{1,0:T(8,128)(2,1)S(1)} collective-permute-done((bf16[128,2048]{1,0:T(8,128)(2,1)S(1)}, bf16[128,2048]{1,0:T(8,128)(2,1)S(1)}, u32[]{:S(2)}, u32[]{:S(2)}) %collective-permute-start.7) | collective-permute-done | bytes 524320 | tf_op jit(solution)/shard_map/ppermute | solution.py:330
  44.7 1.6 %shard_map.123.refs_2_ = f32[512,768]{1,0:T(8,128)S(1)} custom-call(s32[5]{0:T(128)S(1)} %dynamic-slice_bitcast_fusion.order_ref, bf16[128,2176]{1,0:T(8,128)(2,1)S(1)} %shard_map.119.refs_0_, bf16[128,2176]{1,0:T(8,128)(2,1)S(1)} %collective-permute-done.refs_1_, bf16[128,2176]{1,0:T(8,128)(2,1)S(1)} %collective-permute-done.1.refs_2_, ...), custom_call_target="tpu_custom_call" | custom-call | flops 11010048 | bytes 46080 | tf_op jit(solution)/shard_map/pallas_call | solution.py:175
  48.8 2.5 %shard_map.126 = (bf16[96,2048]{1,0:T(8,128)(2,1)S(1)}, bf16[96,2048]{1,0:T(8,128)(2,1)S(1)}, bf16[96,2048]{1,0:T(8,128)(2,1)S(1)}, bf16[96,2048]{1,0:T(8,128)(2,1)S(1)}) custom-call(s32[5]{0:T(128)S(1)} %dynamic-slice_bitcast_fusion.order_ref, bf16[768,384]{1,0:T(8,128)(2,1)S(1)} %get-tuple-element.90.refs_0_.refs_4_, ...), custom_call_target="tpu_custom_call" | custom-call | flops 25165824 | bytes 77824 | tf_op jit(solution)/shard_map/pallas_call | solution.py:204
  51.3 1.6 %collective-permute-start.15 = (bf16[96,2048]{1,0:T(8,128)(2,1)S(1)}, bf16[96,2048]{1,0:T(8,128)(2,1)S(1)}, u32[]{:S(2)}, u32[]{:S(2)}) collective-permute-start(bf16[96,2048]{1,0:T(8,128)(2,1)S(1)} %get-tuple-element.83), channel_id=1, source_target_pairs={{0,8},{8,0},{16,24},{24,16},{1,9},{9,1},{17,25},{25,17},{2,10},{10... | collective-permute-start | bytes 1179656 | tf_op jit(solution)/shard_map/ppermute | solution.py:356
  52.9 3.2 %shard_map.127 = (bf16[512,768]{1,0:T(8,128)(2,1)S(1)}, bf16[512,768]{1,0:T(8,128)(2,1)S(1)}, bf16[512,768]{1,0:T(8,128)(2,1)S(1)}) custom-call(s32[5]{0:T(128)S(1)} %dynamic-slice_bitcast_fusion.order_ref, bf16[128,2176]{1,0:T(8,128)(2,1)S(1)} %shard_map.119.refs_0_, bf16[128,2176]{1,0:T(8,128)(2,1)S(1)} %collective-permute-done.refs_1_, ...), custom_call_target="tpu_custom_call" | custom-call | flops 37748736 | bytes 61440 | tf_op jit(solution)/shard_map/pallas_call | solution.py:175
  56.2 3.1 %shard_map.128 = (bf16[512,2048]{1,0:T(8,128)(2,1)S(1)}, bf16[512,2048]{1,0:T(8,128)(2,1)S(1)}) custom-call(s32[1]{0:T(128)} %bitcast.1.me_ref, bf16[128,2176]{1,0:T(8,128)(2,1)S(1)} %collective-permute-done.2.refs_3_.refs_0_, bf16[128,2176]{1,0:T(8,128)(2,1)S(1)} %collective-permute-done.3.refs_4_.refs_1_, ...), custom_call_target="tpu_custom_call" | custom-call | flops 37748736 | bytes 139264 | tf_op jit(solution)/shard_map/pallas_call | solution.py:144
  59.2 17.0 %collective-permute-done.15.refs_1_.down_one = bf16[96,2048]{1,0:T(8,128)(2,1)S(1)} collective-permute-done((bf16[96,2048]{1,0:T(8,128)(2,1)S(1)}, bf16[96,2048]{1,0:T(8,128)(2,1)S(1)}, u32[]{:S(2)}, u32[]{:S(2)}) %collective-permute-start.15) | collective-permute-done | bytes 393248 | tf_op jit(solution)/shard_map/ppermute | solution.py:356
  77.7 2.6 %collective-permute-start.16 = (bf16[2304,256]{1,0:T(8,128)(2,1)S(1)}, bf16[2304,256]{1,0:T(8,128)(2,1)S(1)}, u32[]{:S(2)}, u32[]{:S(2)}) collective-permute-start(bf16[2304,256]{1,0:T(8,128)(2,1)S(1)} %shard_map.129), channel_id=1, source_target_pairs={{0,8},{8,24},{24,16},{16,0},{1,9},{9,25},{25,17},{17,1},{2,10},{10... | collective-permute-start | bytes 3538952 | tf_op jit(solution)/shard_map/ppermute | solution.py:356
  80.3 1.1 collective-permute-done.17.refs_10_
  81.4 3.0 %collective-permute-done.18.refs_11_ = bf16[512,2048]{1,0:T(8,128)(2,1)S(1)} collective-permute-done((bf16[512,2048]{1,0:T(8,128)(2,1)S(1)}, bf16[512,2048]{1,0:T(8,128)(2,1)S(1)}, u32[]{:S(2)}, u32[]{:S(2)}) %collective-permute-start.18) | collective-permute-done | bytes 2097184 | tf_op jit(solution)/shard_map/ppermute | solution.py:330
  84.4 3.0 %shard_map.130 = (bf16[128,2048]{1,0:T(8,128)(2,1)S(1)}, bf16[128,2048]{1,0:T(8,128)(2,1)S(1)}, bf16[256,2048]{1,0:T(8,128)(2,1)S(1)}, bf16[128,2048]{1,0:T(8,12...) custom-call(s32[1]{0:T(128)} %bitcast.1.me_ref, bf16[128,2176]{1,0:T(8,128)(2,1)S(1)} %shard_map.119.refs_0_, ...), custom_call_target="tpu_custom_call" | custom-call | flops 37748736 | bytes 139264 | tf_op jit(solution)/shard_map/pallas_call | solution.py:144
  87.4 1.6 %collective-permute-start.19 = (bf16[256,2048]{1,0:T(8,128)(2,1)S(1)}, bf16[256,2048]{1,0:T(8,128)(2,1)S(1)}, u32[]{:S(2)}, u32[]{:S(2)}) collective-permute-start(bf16[256,2048]{1,0:T(8,128)(2,1)S(1)} %get-tuple-element.100), channel_id=1, source_target_pairs={{0,2},{1,3},{2,0},{3,1},{4,6},{5,7},{6,4},{7,5},{8,10},{9,11},{10,... | collective-permute-start | bytes 3145736 | tf_op jit(solution)/shard_map/ppermute | solution.py:330
  90.1 15.7 %collective-permute-done.16.refs_0_.two_ref = bf16[2304,256]{1,0:T(8,128)(2,1)S(1)} collective-permute-done((bf16[2304,256]{1,0:T(8,128)(2,1)S(1)}, bf16[2304,256]{1,0:T(8,128)(2,1)S(1)}, u32[]{:S(2)}, u32[]{:S(2)}) %collective-permute-start.16) | collective-permute-done | bytes 1179680 | tf_op jit(solution)/shard_map/ppermute | solution.py:356
  106.7 3.4 %collective-permute-start.24 = (bf16[2304,256]{1,0:T(8,128)(2,1)S(1)}, bf16[2304,256]{1,0:T(8,128)(2,1)S(1)}, u32[]{:S(2)}, u32[]{:S(2)}) collective-permute-start(bf16[2304,256]{1,0:T(8,128)(2,1)S(1)} %shard_map.132), channel_id=1, source_target_pairs={{8,16},{16,8},{9,17},{17,9},{10,18},{18,10},{11,19},{19,11},{12,20... | collective-permute-start | bytes 3538952 | tf_op jit(solution)/shard_map/ppermute | solution.py:356
  110.1 1.3 collective-permute-start.23
  111.4 1.3 collective-permute-done.19.refs_1_
  112.6 1.2 collective-permute-done.20.refs_3_.refs_4_
  116.2 10.8 %collective-permute-done.21.refs_2_ = bf16[128,2048]{1,0:T(8,128)(2,1)S(1)} collective-permute-done((bf16[128,2048]{1,0:T(8,128)(2,1)S(1)}, bf16[128,2048]{1,0:T(8,128)(2,1)S(1)}, u32[]{:S(2)}, u32[]{:S(2)}) %collective-permute-start.21) | collective-permute-done | bytes 524320 | tf_op jit(solution)/shard_map/ppermute | solution.py:330
  127.2 1.3 shard_map.135
  128.5 7.2 %collective-permute-done.24.low_ref = bf16[2304,256]{1,0:T(8,128)(2,1)S(1)} collective-permute-done((bf16[2304,256]{1,0:T(8,128)(2,1)S(1)}, bf16[2304,256]{1,0:T(8,128)(2,1)S(1)}, u32[]{:S(2)}, u32[]{:S(2)}) %collective-permute-start.24) | collective-permute-done | bytes 1179680 | tf_op jit(solution)/shard_map/ppermute | solution.py:356
  135.7 3.1 %collective-permute-done.23.up_ref = bf16[2304,256]{1,0:T(8,128)(2,1)S(1)} collective-permute-done((bf16[2304,256]{1,0:T(8,128)(2,1)S(1)}, bf16[2304,256]{1,0:T(8,128)(2,1)S(1)}, u32[]{:S(2)}, u32[]{:S(2)}) %collective-permute-start.23) | collective-permute-done | bytes 1179680 | tf_op jit(solution)/shard_map/ppermute | solution.py:356
  138.8 1.6 %shard_map.136 = (f32[512,384]{1,0:T(8,128)}, f32[512,384]{1,0:T(8,128)}, f32[96,2048]{1,0:T(8,128)}) custom-call(f32[512,768]{1,0:T(8,128)S(1)} %get-tuple-element.118.wide_ref, f32[96,2048]{1,0:T(8,128)S(1)} %get-tuple-element.119.down_ref, bf16[2304,256]{1,0:T(8,128)(2,1)S(1)} %collective-permute-done.23.up_ref, ...), custom_call_target="tpu_custom_call" | custom-call | flops 6144 | bytes 36864 | tf_op jit(solution)/shard_map/pallas_call | solution.py:283
  (49 shorter events, 16.6 us)
Async XLA Ops:
  0.6 15.1 %collective-permute-start.8 = (bf16[128,2048]{1,0:T(8,128)(2,1)}, bf16[128,2048]{1,0:T(8,128)(2,1)S(1)}, u32[]{:S(2)}, u32[]{:S(2)}) collective-permute-start(bf16[128,2048]{1,0:T(8,128)(2,1)} %refs_6_.1), channel_id=1, source_target_pairs={{0,2},{1,3},{2,0},{3,1},{4,6},{5,7},{6,4},{7,5},{8,10},{9,11},{10,... | collective-permute-start | bytes 1572872 | tf_op jit(solution)/shard_map/ppermute | solution.py:330
  1.2 15.1 %collective-permute-start.6 = (bf16[128,2048]{1,0:T(8,128)(2,1)}, bf16[128,2048]{1,0:T(8,128)(2,1)S(1)}, u32[]{:S(2)}, u32[]{:S(2)}) collective-permute-start(bf16[128,2048]{1,0:T(8,128)(2,1)} %refs_6_.1), channel_id=1, source_target_pairs={{0,4},{1,5},{2,6},{3,7},{4,0},{5,1},{6,2},{7,3},{8,12},{9,13},{10,... | collective-permute-start | bytes 1572872 | tf_op jit(solution)/shard_map/ppermute | solution.py:330
  5.0 1.0 copy-start.4
  6.3 20.5 %collective-permute-start.1 = (bf16[128,2176]{1,0:T(8,128)(2,1)S(1)}, bf16[128,2176]{1,0:T(8,128)(2,1)S(1)}, u32[]{:S(2)}, u32[]{:S(2)}) collective-permute-start(bf16[128,2176]{1,0:T(8,128)(2,1)S(1)} %shard_map.119.refs_0_), channel_id=1, source_target_pairs={{0,4},{1,5},{2,6},{3,7},{4,0},{5,1},{6,2},{7,3},{8,12},{9,13},{10,... | collective-permute-start | bytes 1671176 | tf_op jit(solution)/shard_map/ppermute | solution.py:330
  6.8 19.9 %collective-permute-start = (bf16[128,2176]{1,0:T(8,128)(2,1)S(1)}, bf16[128,2176]{1,0:T(8,128)(2,1)S(1)}, u32[]{:S(2)}, u32[]{:S(2)}) collective-permute-start(bf16[128,2176]{1,0:T(8,128)(2,1)S(1)} %shard_map.119.refs_0_), channel_id=1, source_target_pairs={{0,2},{1,3},{2,0},{3,1},{4,6},{5,7},{6,4},{7,5},{8,10},{9,11},{10,... | collective-permute-start | bytes 1671176 | tf_op jit(solution)/shard_map/ppermute | solution.py:330
  8.3 20.5 %collective-permute-start.2 = (bf16[128,2176]{1,0:T(8,128)(2,1)S(1)}, bf16[128,2176]{1,0:T(8,128)(2,1)S(1)}, u32[]{:S(2)}, u32[]{:S(2)}) collective-permute-start(bf16[128,2176]{1,0:T(8,128)(2,1)S(1)} %shard_map.119.refs_0_), channel_id=1, source_target_pairs={{0,1},{1,0},{2,3},{3,2},{4,5},{5,4},{6,7},{7,6},{8,9},{9,8},{10,11... | collective-permute-start | bytes 1671176 | tf_op jit(solution)/shard_map/ppermute | solution.py:330
  8.3 1.4 %copy-start = (bf16[1,2048,384]{2,1,0:T(8,128)(2,1)S(1)}, bf16[1,2048,384]{2,1,0:T(8,128)(2,1)}, u32[]{:S(2)}) copy-start(bf16[1,2048,384]{2,1,0:T(8,128)(2,1)} %param.11) | copy-start | bytes 4718596
  9.7 1.4 %copy-start.1 = (bf16[1,2048,384]{2,1,0:T(8,128)(2,1)S(1)}, bf16[1,2048,384]{2,1,0:T(8,128)(2,1)}, u32[]{:S(2)}) copy-start(bf16[1,2048,384]{2,1,0:T(8,128)(2,1)} %param.12) | copy-start | bytes 4718596
  11.1 1.4 %copy-start.2 = (bf16[1,384,2048]{2,1,0:T(8,128)(2,1)S(1)}, bf16[1,384,2048]{2,1,0:T(8,128)(2,1)}, u32[]{:S(2)}) copy-start(bf16[1,384,2048]{2,1,0:T(8,128)(2,1)} %param.13) | copy-start | bytes 4718596
  12.5 3.2 %copy-start.3 = (bf16[128,2048]{1,0:T(8,128)(2,1)S(1)}, bf16[128,2048]{1,0:T(8,128)(2,1)}, u32[]{:S(2)}) copy-start(bf16[128,2048]{1,0:T(8,128)(2,1)} %refs_6_.1) | copy-start | bytes 1572868
  15.7 11.6 %collective-permute-start.9 = (bf16[128,2048]{1,0:T(8,128)(2,1)S(1)}, bf16[128,2048]{1,0:T(8,128)(2,1)S(1)}, u32[]{:S(2)}, u32[]{:S(2)}) collective-permute-start(bf16[128,2048]{1,0:T(8,128)(2,1)S(1)} %copy-done.3), channel_id=1, source_target_pairs={{0,1},{1,0},{2,3},{3,2},{4,5},{5,4},{6,7},{7,6},{8,9},{9,8},{10,11... | collective-permute-start | bytes 1572872 | tf_op jit(solution)/shard_map/ppermute | solution.py:330
  16.3 12.5 %collective-permute-start.10 = (bf16[128,2048]{1,0:T(8,128)(2,1)S(1)}, bf16[128,2048]{1,0:T(8,128)(2,1)S(1)}, u32[]{:S(2)}, u32[]{:S(2)}) collective-permute-start(bf16[128,2048]{1,0:T(8,128)(2,1)S(1)} %collective-permute-done.8.refs_7_), channel_id=1, source_target_pairs={{0,1},{1,0},{2,3},{3,2},{4,5},{5,4},{6,7},{7,6},{8,9},{9,8},{10,11... | collective-permute-start | bytes 1572872 | tf_op jit(solution)/shard_map/ppermute | solution.py:330
  26.8 4.0 %collective-permute-start.4 = (bf16[128,2176]{1,0:T(8,128)(2,1)S(1)}, bf16[128,2176]{1,0:T(8,128)(2,1)S(1)}, u32[]{:S(2)}, u32[]{:S(2)}) collective-permute-start(bf16[128,2176]{1,0:T(8,128)(2,1)S(1)} %collective-permute-done.1.refs_2_), channel_id=1, source_target_pairs={{0,1},{1,0},{2,3},{3,2},{4,5},{5,4},{6,7},{7,6},{8,9},{9,8},{10,11... | collective-permute-start | bytes 1671176 | tf_op jit(solution)/shard_map/ppermute | solution.py:330
  26.8 4.0 %collective-permute-start.3 = (bf16[128,2176]{1,0:T(8,128)(2,1)S(1)}, bf16[128,2176]{1,0:T(8,128)(2,1)S(1)}, u32[]{:S(2)}, u32[]{:S(2)}) collective-permute-start(bf16[128,2176]{1,0:T(8,128)(2,1)S(1)} %collective-permute-done.refs_1_), channel_id=1, source_target_pairs={{0,1},{1,0},{2,3},{3,2},{4,5},{5,4},{6,7},{7,6},{8,9},{9,8},{10,11... | collective-permute-start | bytes 1671176 | tf_op jit(solution)/shard_map/ppermute | solution.py:330
  27.3 15.9 %collective-permute-start.5 = (bf16[128,2176]{1,0:T(8,128)(2,1)S(1)}, bf16[128,2176]{1,0:T(8,128)(2,1)S(1)}, u32[]{:S(2)}, u32[]{:S(2)}) collective-permute-start(bf16[128,2176]{1,0:T(8,128)(2,1)S(1)} %collective-permute-done.refs_1_), channel_id=1, source_target_pairs={{0,4},{1,5},{2,6},{3,7},{4,0},{5,1},{6,2},{7,3},{8,12},{9,13},{10,... | collective-permute-start | bytes 1671176 | tf_op jit(solution)/shard_map/ppermute | solution.py:330
  28.8 1.9 %collective-permute-start.11 = (bf16[128,2048]{1,0:T(8,128)(2,1)S(1)}, bf16[128,2048]{1,0:T(8,128)(2,1)S(1)}, u32[]{:S(2)}, u32[]{:S(2)}) collective-permute-start(bf16[128,2048]{1,0:T(8,128)(2,1)S(1)} %collective-permute-done.6.refs_8_), channel_id=1, source_target_pairs={{0,1},{1,0},{2,3},{3,2},{4,5},{5,4},{6,7},{7,6},{8,9},{9,8},{10,11... | collective-permute-start | bytes 1572872 | tf_op jit(solution)/shard_map/ppermute | solution.py:330
  28.8 14.3 %collective-permute-start.7 = (bf16[128,2048]{1,0:T(8,128)(2,1)S(1)}, bf16[128,2048]{1,0:T(8,128)(2,1)S(1)}, u32[]{:S(2)}, u32[]{:S(2)}) collective-permute-start(bf16[128,2048]{1,0:T(8,128)(2,1)S(1)} %collective-permute-done.6.refs_8_), channel_id=1, source_target_pairs={{0,2},{1,3},{2,0},{3,1},{4,6},{5,7},{6,4},{7,5},{8,10},{9,11},{10,... | collective-permute-start | bytes 1572872 | tf_op jit(solution)/shard_map/ppermute | solution.py:330
  43.2 3.1 %collective-permute-start.12 = (bf16[128,2176]{1,0:T(8,128)(2,1)S(1)}, bf16[128,2176]{1,0:T(8,128)(2,1)S(1)}, u32[]{:S(2)}, u32[]{:S(2)}) collective-permute-start(bf16[128,2176]{1,0:T(8,128)(2,1)S(1)} %collective-permute-done.5.refs_0_.refs_6_.refs_3_), channel_id=1, source_target_pairs={{0,1},{1,0},{2,3},{3,2},{4,5},{5,4},{6,7},{7,6},{8,9},{9,8},{10,11... | collective-permute-start | bytes 1671176 | tf_op jit(solution)/shard_map/ppermute | solution.py:330
  43.2 3.1 %collective-permute-start.13 = (bf16[128,2048]{1,0:T(8,128)(2,1)S(1)}, bf16[128,2048]{1,0:T(8,128)(2,1)S(1)}, u32[]{:S(2)}, u32[]{:S(2)}) collective-permute-start(bf16[128,2048]{1,0:T(8,128)(2,1)S(1)} %collective-permute-done.7.refs_1_), channel_id=1, source_target_pairs={{0,1},{1,0},{2,3},{3,2},{4,5},{5,4},{6,7},{7,6},{8,9},{9,8},{10,11... | collective-permute-start | bytes 1572872 | tf_op jit(solution)/shard_map/ppermute | solution.py:330
  48.3 27.9 %collective-permute-start.14 = (bf16[512,768]{1,0:T(8,128)(2,1)S(1)}, bf16[512,768]{1,0:T(8,128)(2,1)S(1)}, u32[]{:S(2)}, u32[]{:S(2)}) collective-permute-start(bf16[512,768]{1,0:T(8,128)(2,1)S(1)} %shard_map.125), channel_id=1, source_target_pairs={{0,8},{8,0},{16,24},{24,16},{1,9},{9,1},{17,25},{25,17},{2,10},{10... | collective-permute-start | bytes 2359304 | tf_op jit(solution)/shard_map/ppermute | solution.py:356
  51.3 25.0 %collective-permute-start.15 = (bf16[96,2048]{1,0:T(8,128)(2,1)S(1)}, bf16[96,2048]{1,0:T(8,128)(2,1)S(1)}, u32[]{:S(2)}, u32[]{:S(2)}) collective-permute-start(bf16[96,2048]{1,0:T(8,128)(2,1)S(1)} %get-tuple-element.83), channel_id=1, source_target_pairs={{0,8},{8,0},{16,24},{24,16},{1,9},{9,1},{17,25},{25,17},{2,10},{10... | collective-permute-start | bytes 1179656 | tf_op jit(solution)/shard_map/ppermute | solution.py:356
  77.1 4.2 %collective-permute-start.17 = (bf16[512,2048]{1,0:T(8,128)(2,1)S(1)}, bf16[512,2048]{1,0:T(8,128)(2,1)S(1)}, u32[]{:S(2)}, u32[]{:S(2)}) collective-permute-start(bf16[512,2048]{1,0:T(8,128)(2,1)S(1)} %get-tuple-element.96), channel_id=1, source_target_pairs={{0,1},{1,0},{2,3},{3,2},{4,5},{5,4},{6,7},{7,6},{8,9},{9,8},{10,11... | collective-permute-start | bytes 6291464 | tf_op jit(solution)/shard_map/ppermute | solution.py:330
  77.2 7.1 %collective-permute-start.18 = (bf16[512,2048]{1,0:T(8,128)(2,1)S(1)}, bf16[512,2048]{1,0:T(8,128)(2,1)S(1)}, u32[]{:S(2)}, u32[]{:S(2)}) collective-permute-start(bf16[512,2048]{1,0:T(8,128)(2,1)S(1)} %get-tuple-element.97), channel_id=1, source_target_pairs={{0,1},{1,0},{2,3},{3,2},{4,5},{5,4},{6,7},{7,6},{8,9},{9,8},{10,11... | collective-permute-start | bytes 6291464 | tf_op jit(solution)/shard_map/ppermute | solution.py:330
  77.7 28.1 %collective-permute-start.16 = (bf16[2304,256]{1,0:T(8,128)(2,1)S(1)}, bf16[2304,256]{1,0:T(8,128)(2,1)S(1)}, u32[]{:S(2)}, u32[]{:S(2)}) collective-permute-start(bf16[2304,256]{1,0:T(8,128)(2,1)S(1)} %shard_map.129), channel_id=1, source_target_pairs={{0,8},{8,24},{24,16},{16,0},{1,9},{9,25},{25,17},{17,1},{2,10},{10... | collective-permute-start | bytes 3538952 | tf_op jit(solution)/shard_map/ppermute | solution.py:356
  87.4 25.3 %collective-permute-start.19 = (bf16[256,2048]{1,0:T(8,128)(2,1)S(1)}, bf16[256,2048]{1,0:T(8,128)(2,1)S(1)}, u32[]{:S(2)}, u32[]{:S(2)}) collective-permute-start(bf16[256,2048]{1,0:T(8,128)(2,1)S(1)} %get-tuple-element.100), channel_id=1, source_target_pairs={{0,2},{1,3},{2,0},{3,1},{4,6},{5,7},{6,4},{7,5},{8,10},{9,11},{10,... | collective-permute-start | bytes 3145736 | tf_op jit(solution)/shard_map/ppermute | solution.py:330
  88.9 24.9 %collective-permute-start.20 = (bf16[256,2048]{1,0:T(8,128)(2,1)S(1)}, bf16[256,2048]{1,0:T(8,128)(2,1)S(1)}, u32[]{:S(2)}, u32[]{:S(2)}) collective-permute-start(bf16[256,2048]{1,0:T(8,128)(2,1)S(1)} %get-tuple-element.103), channel_id=1, source_target_pairs={{0,4},{1,5},{2,6},{3,7},{4,0},{5,1},{6,2},{7,3},{8,12},{9,13},{10,... | collective-permute-start | bytes 3145736 | tf_op jit(solution)/shard_map/ppermute | solution.py:330
  106.7 29.0 %collective-permute-start.24 = (bf16[2304,256]{1,0:T(8,128)(2,1)S(1)}, bf16[2304,256]{1,0:T(8,128)(2,1)S(1)}, u32[]{:S(2)}, u32[]{:S(2)}) collective-permute-start(bf16[2304,256]{1,0:T(8,128)(2,1)S(1)} %shard_map.132), channel_id=1, source_target_pairs={{8,16},{16,8},{9,17},{17,9},{10,18},{18,10},{11,19},{19,11},{12,20... | collective-permute-start | bytes 3538952 | tf_op jit(solution)/shard_map/ppermute | solution.py:356
  110.1 28.7 %collective-permute-start.23 = (bf16[2304,256]{1,0:T(8,128)(2,1)S(1)}, bf16[2304,256]{1,0:T(8,128)(2,1)S(1)}, u32[]{:S(2)}, u32[]{:S(2)}) collective-permute-start(bf16[2304,256]{1,0:T(8,128)(2,1)S(1)} %shard_map.131), channel_id=1, source_target_pairs={{0,8},{24,16},{1,9},{25,17},{2,10},{26,18},{3,11},{27,19},{4,12},{... | collective-permute-start | bytes 3538952 | tf_op jit(solution)/shard_map/ppermute | solution.py:356
  114.1 12.9 %collective-permute-start.21 = (bf16[128,2048]{1,0:T(8,128)(2,1)S(1)}, bf16[128,2048]{1,0:T(8,128)(2,1)S(1)}, u32[]{:S(2)}, u32[]{:S(2)}) collective-permute-start(bf16[128,2048]{1,0:T(8,128)(2,1)S(1)} %get-tuple-element.109), channel_id=1, source_target_pairs={{0,4},{1,5},{2,6},{3,7},{4,0},{5,1},{6,2},{7,3},{8,12},{9,13},{10,... | collective-permute-start | bytes 1572872 | tf_op jit(solution)/shard_map/ppermute | solution.py:330
  114.7 12.5 %collective-permute-start.22 = (bf16[128,2048]{1,0:T(8,128)(2,1)S(1)}, bf16[128,2048]{1,0:T(8,128)(2,1)S(1)}, u32[]{:S(2)}, u32[]{:S(2)}) collective-permute-start(bf16[128,2048]{1,0:T(8,128)(2,1)S(1)} %get-tuple-element.110), channel_id=1, source_target_pairs={{0,2},{1,3},{2,0},{3,1},{4,6},{5,7},{6,4},{7,5},{8,10},{9,11},{10,... | collective-permute-start | bytes 1572872 | tf_op jit(solution)/shard_map/ppermute | solution.py:330
where the time goes:
time: 142 us; the launch traced here: 140 us
  waiting for transfers between devices  82.7 us (58%)
  Pallas kernels  27.9 us (20%)
  starting transfers between devices  21.4 us (15%)
  local copies, waits for them, and re-layouts  7.54 us (5%)
    ppermute x5, waiting for transfers between devices, move(): return lax.ppermute(array, 'dp', pairs) if line else array  43 us
    ppermute x20, waiting for transfers between devices, flip(): return lax.ppermute(array, 'expert', [(i, i ^ bit) for i in range(group)])  39.7 us
    ppermute x20, starting transfers between devices, flip(): return lax.ppermute(array, 'expert', [(i, i ^ bit) for i in range(group)])  12 us
    ppermute x5, starting transfers between devices, move(): return lax.ppermute(array, 'dp', pairs) if line else array  9.42 us
    unnamed x12, local copies, waits for them, and re-layouts  6.86 us
    pallas_call x3, Pallas kernels, hidden(): pl.pallas_call(functools.partial(hidden_kernel, blocks), out_shape=outs,...  6.56 us
    pallas_call x2, Pallas kernels, rows_out(): pl.pallas_call(functools.partial(rows_kernel, blocks, groups, part, place...  6.09 us
    pallas_call x3, Pallas kernels, wide_grads(): pl.pallas_call(functools.partial(wide_grad_kernel, blocks, len(hids), fir...  5.75 us
  transfers between devices with their start and end apart: 25, of which 15 were waited for; matrix products, arithmetic and copies ran while one was open for 2% of the time, Pallas kernels for 17%

commit v1 on v0

--- a/solution.py
+++ b/solution.py
@@ -344,12 +344,11 @@
     cots_a += [flip(c, CORE) for c in [after(cot_0, wide_panel)] + cots_a[1:]]
     toks_a += [flip(t, CORE) for t in toks_a]
     act_a, hid_a, og_a = hidden(me, toks_a, cots_a, wide_panel, down_panel)
-    tok_d, cot_d = after((tok_d, cot_d), act_a)
+    (wide_part,) = wide_grads(order, toks_a, (hid_a,), width, 0, 1, kind=F32)
+    tok_d, cot_d = after((tok_d, cot_d), wide_part)
     tok_e, cot_e = flip(tok_d, CORE), flip(cot_d, CORE)
     act_d, hid_d, og_d = hidden(me, [tok_d], [cot_d], wide_panel, down_panel)
-    toks = toks_a + [tok_d]
-    (wide_part,) = wide_grads(order, toks, (hid_a, hid_d), width, 0, 1, kind=F32)
-    tok_e, cot_e = after((tok_e, cot_e), wide_part)
+    tok_e, cot_e = after((tok_e, cot_e), hid_d)
     act_e, hid_e, og_e = hidden(me, [tok_e], [cot_e], wide_panel, down_panel)
 
     def move(array, pairs):
@@ -358,8 +357,8 @@
     one_pairs = [(0, 1), (1, 0), (2, 3), (3, 2)]
     two_pairs = [(0, 1), (1, 3), (3, 2), (2, 0)]
     end_pairs, mid_pairs = [(0, 1), (3, 2)], [(1, 2), (2, 1)]
-    toks = toks + [tok_e]
-    wide_0 = wide_grads(order, [tok_e], (hid_e,), width, 0, 1, start=(wide_part,))
+    toks = toks_a + [tok_d, tok_e]
+    wide_0 = wide_grads(order, [tok_d, tok_e], (hid_d, hid_e), width, 0, 1, start=(wide_part,))
     wide_one = move(wide_0[0], one_pairs)
     act_a = after(act_a, wide_0)
     down = down_grads(order, (act_a, act_d, act_e), (og_a, og_d, og_e))
@@ -385,7 +384,7 @@
         own_last = join(order, *after((wide[2], down[2]), kept))
         two = after(two, own_last)
         last = join(order, wide[2], down[2], two)
-        last_end, last_mid = move(own_last, end_pairs), move(last, mid_pairs)
+        last_mid, last_end = move(last, mid_pairs), move(own_last, end_pairs)
         out_near, grad_far = after((out_near, grad_far), last)
     out_y, grad_x = pair_sums(each, [(out_y, 0), (out_near, 1)], [(grad_x, 0), (grad_far, 1)])
     out_yy, grad_xx = flip(out_y, FAR), flip(grad_x, NEAR)
@@ -396,8 +395,9 @@
     )
     if line:
         base, mixed, grad_tokens = lax.optimization_barrier((base, mixed, grad_tokens))
-        last_end, last_mid = after((last_end, last_mid), (mixed, grad_tokens))
-        grad_gate, grad_up, grad_down = finish(*base, last_end, last_mid)
+        last_end = after(last_end, (mixed, grad_tokens))
+        last_mid = after(last_mid, last_end)
+        grad_gate, grad_up, grad_down = finish(*base, last_mid, last_end)
     else:
         wide_all = jnp.concatenate(wide, axis=0)
         grad_wide = lax.psum_scatter(wide_all, "dp", scatter_dimension=0, tiled=True).astype(F32)

time: 142 us -> 138 us (0.972)
  waiting for transfers between devices: 82.7 us -> 79.4 us
    ppermute x5, waiting for transfers between devices: 43 us -> 39.5 us  [move(): return lax.ppermute(array, 'dp', pairs) if line else array]
  transfers between devices with their start and end apart: 25 -> 25, of which waited for: 15 -> 16; matrix products, arithmetic and copies ran while one was open for 2% -> 2% of each run, Pallas kernels for 17% -> 17%
where the time goes in v1:
time: 138 us; the launch traced here: 137 us
  waiting for transfers between devices  79.4 us (58%)
  Pallas kernels  27.8 us (20%)
  starting transfers between devices  21.5 us (16%)
  local copies, waits for them, and re-layouts  7.54 us (5%)
    ppermute x20, waiting for transfers between devices, flip(): return lax.ppermute(array, 'expert', [(i, i ^ bit) for i in range(group)])  39.9 us
    ppermute x5, waiting for transfers between devices, move(): return lax.ppermute(array, 'dp', pairs) if line else array  39.5 us
    ppermute x20, starting transfers between devices, flip(): return lax.ppermute(array, 'expert', [(i, i ^ bit) for i in range(group)])  12 us
    ppermute x5, starting transfers between devices, move(): return lax.ppermute(array, 'dp', pairs) if line else array  9.52 us
    unnamed x12, local copies, waits for them, and re-layouts  6.86 us
    pallas_call x3, Pallas kernels, hidden(): pl.pallas_call(functools.partial(hidden_kernel, blocks), out_shape=outs,...  6.56 us
    pallas_call x2, Pallas kernels, rows_out(): pl.pallas_call(functools.partial(rows_kernel, blocks, groups, part, place...  6.09 us
    pallas_call x3, Pallas kernels, wide_grads(): pl.pallas_call(functools.partial(wide_grad_kernel, blocks, len(hids), fir...  5.56 us
  transfers between devices with their start and end apart: 25, of which 16 were waited for; matrix products, arithmetic and copies ran while one was open for 2% of the time, Pallas kernels for 17%

profile of v1, /device:TPU:10, one launch (start us, length us, event | category | flops | bytes accessed | tf_op | source)
XLA Modules:
  0.0 137.1 jit_solution(12934865468279335857)
XLA Ops:
  1.2 1.5 %collective-permute-start.6 = (bf16[128,2048]{1,0:T(8,128)(2,1)}, bf16[128,2048]{1,0:T(8,128)(2,1)S(1)}, u32[]{:S(2)}, u32[]{:S(2)}) collective-permute-start(bf16[128,2048]{1,0:T(8,128)(2,1)} %refs_6_.1), channel_id=1, source_target_pairs={{0,4},{1,5},{2,6},{3,7},{4,0},{5,1},{6,2},{7,3},{8,12},{9,13},{10,... | collective-permute-start | bytes 1572872 | tf_op jit(solution)/shard_map/ppermute | solution.py:330
  6.8 1.5 %collective-permute-start = (bf16[128,2176]{1,0:T(8,128)(2,1)S(1)}, bf16[128,2176]{1,0:T(8,128)(2,1)S(1)}, u32[]{:S(2)}, u32[]{:S(2)}) collective-permute-start(bf16[128,2176]{1,0:T(8,128)(2,1)S(1)} %shard_map.119.refs_0_), channel_id=1, source_target_pairs={{0,2},{1,3},{2,0},{3,1},{4,6},{5,7},{6,4},{7,5},{8,10},{9,11},{10,... | collective-permute-start | bytes 1671176 | tf_op jit(solution)/shard_map/ppermute | solution.py:330
  8.3 1.4 %copy-done = bf16[1,2048,384]{2,1,0:T(8,128)(2,1)S(1)} copy-done((bf16[1,2048,384]{2,1,0:T(8,128)(2,1)S(1)}, bf16[1,2048,384]{2,1,0:T(8,128)(2,1)}, u32[]{:S(2)}) %copy-start) | copy-done | bytes 1572888
  9.7 1.4 %copy-done.1 = bf16[1,2048,384]{2,1,0:T(8,128)(2,1)S(1)} copy-done((bf16[1,2048,384]{2,1,0:T(8,128)(2,1)S(1)}, bf16[1,2048,384]{2,1,0:T(8,128)(2,1)}, u32[]{:S(2)}) %copy-start.1) | copy-done | bytes 1572888
  11.1 1.4 %copy-done.2 = bf16[1,384,2048]{2,1,0:T(8,128)(2,1)S(1)} copy-done((bf16[1,384,2048]{2,1,0:T(8,128)(2,1)S(1)}, bf16[1,384,2048]{2,1,0:T(8,128)(2,1)}, u32[]{:S(2)}) %copy-start.2) | copy-done | bytes 1572888
  12.9 2.8 %collective-permute-done.8.refs_7_ = bf16[128,2048]{1,0:T(8,128)(2,1)S(1)} collective-permute-done((bf16[128,2048]{1,0:T(8,128)(2,1)}, bf16[128,2048]{1,0:T(8,128)(2,1)S(1)}, u32[]{:S(2)}, u32[]{:S(2)}) %collective-permute-start.8) | collective-permute-done | bytes 524320 | tf_op jit(solution)/shard_map/ppermute | solution.py:330
  16.3 10.5 %collective-permute-done.1.refs_2_ = bf16[128,2176]{1,0:T(8,128)(2,1)S(1)} collective-permute-done((bf16[128,2176]{1,0:T(8,128)(2,1)S(1)}, bf16[128,2176]{1,0:T(8,128)(2,1)S(1)}, u32[]{:S(2)}, u32[]{:S(2)}) %collective-permute-start.1) | collective-permute-done | bytes 557088 | tf_op jit(solution)/shard_map/ppermute | solution.py:330
  27.3 1.5 %collective-permute-start.5 = (bf16[128,2176]{1,0:T(8,128)(2,1)S(1)}, bf16[128,2176]{1,0:T(8,128)(2,1)S(1)}, u32[]{:S(2)}, u32[]{:S(2)}) collective-permute-start(bf16[128,2176]{1,0:T(8,128)(2,1)S(1)} %collective-permute-done.refs_1_), channel_id=1, source_target_pairs={{0,4},{1,5},{2,6},{3,7},{4,0},{5,1},{6,2},{7,3},{8,12},{9,13},{10,... | collective-permute-start | bytes 1671176 | tf_op jit(solution)/shard_map/ppermute | solution.py:330
  28.8 1.6 %collective-permute-start.7 = (bf16[128,2048]{1,0:T(8,128)(2,1)S(1)}, bf16[128,2048]{1,0:T(8,128)(2,1)S(1)}, u32[]{:S(2)}, u32[]{:S(2)}) collective-permute-start(bf16[128,2048]{1,0:T(8,128)(2,1)S(1)} %collective-permute-done.6.refs_8_), channel_id=1, source_target_pairs={{0,2},{1,3},{2,0},{3,1},{4,6},{5,7},{6,4},{7,5},{8,10},{9,11},{10,... | collective-permute-start | bytes 1572872 | tf_op jit(solution)/shard_map/ppermute | solution.py:330
  30.7 4.5 %shard_map.121 = (bf16[768,384]{1,0:T(8,128)(2,1)S(1)}, bf16[768,768]{1,0:T(8,128)(2,1)S(1)}, bf16[768,2048]{1,0:T(8,128)(2,1)S(1)}) custom-call(s32[1]{0:T(128)} %bitcast.1.me_ref, bf16[128,2176]{1,0:T(8,128)(2,1)S(1)} %shard_map.119.refs_0_, bf16[128,2176]{1,0:T(8,128)(2,1)S(1)} %collective-permute-done.refs_1_, ...), custom_call_target="tpu_custom_call" | custom-call | flops 56623104 | bytes 251904 | tf_op jit(solution)/shard_map/pallas_call | solution.py:95
  35.2 1.4 shard_map.122.refs_4_
  36.6 6.6 %collective-permute-done.7.refs_1_ = bf16[128,2048]{1,0:T(8,128)(2,1)S(1)} collective-permute-done((bf16[128,2048]{1,0:T(8,128)(2,1)S(1)}, bf16[128,2048]{1,0:T(8,128)(2,1)S(1)}, u32[]{:S(2)}, u32[]{:S(2)}) %collective-permute-start.7) | collective-permute-done | bytes 524320 | tf_op jit(solution)/shard_map/ppermute | solution.py:330
  44.7 1.2 collective-permute-done.13.refs_1_
  48.4 2.4 %shard_map.126 = (bf16[96,2048]{1,0:T(8,128)(2,1)S(1)}, bf16[96,2048]{1,0:T(8,128)(2,1)S(1)}, bf16[96,2048]{1,0:T(8,128)(2,1)S(1)}, bf16[96,2048]{1,0:T(8,128)(2,1)S(1)}) custom-call(s32[5]{0:T(128)S(1)} %dynamic-slice_bitcast_fusion.order_ref, bf16[768,384]{1,0:T(8,128)(2,1)S(1)} %get-tuple-element.90.refs_0_.refs_4_, ...), custom_call_target="tpu_custom_call" | custom-call | flops 25165824 | bytes 77824 | tf_op jit(solution)/shard_map/pallas_call | solution.py:204
  50.8 1.6 %collective-permute-start.15 = (bf16[96,2048]{1,0:T(8,128)(2,1)S(1)}, bf16[96,2048]{1,0:T(8,128)(2,1)S(1)}, u32[]{:S(2)}, u32[]{:S(2)}) collective-permute-start(bf16[96,2048]{1,0:T(8,128)(2,1)S(1)} %get-tuple-element.83), channel_id=1, source_target_pairs={{0,8},{8,0},{16,24},{24,16},{1,9},{9,1},{17,25},{25,17},{2,10},{10... | collective-permute-start | bytes 1179656 | tf_op jit(solution)/shard_map/ppermute | solution.py:355
  52.5 3.2 %shard_map.127 = (bf16[512,768]{1,0:T(8,128)(2,1)S(1)}, bf16[512,768]{1,0:T(8,128)(2,1)S(1)}, bf16[512,768]{1,0:T(8,128)(2,1)S(1)}) custom-call(s32[5]{0:T(128)S(1)} %dynamic-slice_bitcast_fusion.order_ref, bf16[128,2176]{1,0:T(8,128)(2,1)S(1)} %shard_map.119.refs_0_, bf16[128,2176]{1,0:T(8,128)(2,1)S(1)} %collective-permute-done.refs_1_, ...), custom_call_target="tpu_custom_call" | custom-call | flops 37748736 | bytes 61440 | tf_op jit(solution)/shard_map/pallas_call | solution.py:175
  55.7 3.1 %shard_map.128 = (bf16[512,2048]{1,0:T(8,128)(2,1)S(1)}, bf16[512,2048]{1,0:T(8,128)(2,1)S(1)}) custom-call(s32[1]{0:T(128)} %bitcast.1.me_ref, bf16[128,2176]{1,0:T(8,128)(2,1)S(1)} %collective-permute-done.2.refs_3_.refs_0_, bf16[128,2176]{1,0:T(8,128)(2,1)S(1)} %collective-permute-done.3.refs_4_.refs_1_, ...), custom_call_target="tpu_custom_call" | custom-call | flops 37748736 | bytes 139264 | tf_op jit(solution)/shard_map/pallas_call | solution.py:144
  58.8 17.2 %collective-permute-done.15.refs_1_.down_one = bf16[96,2048]{1,0:T(8,128)(2,1)S(1)} collective-permute-done((bf16[96,2048]{1,0:T(8,128)(2,1)S(1)}, bf16[96,2048]{1,0:T(8,128)(2,1)S(1)}, u32[]{:S(2)}, u32[]{:S(2)}) %collective-permute-start.15) | collective-permute-done | bytes 393248 | tf_op jit(solution)/shard_map/ppermute | solution.py:355
  77.4 2.6 %collective-permute-start.16 = (bf16[2304,256]{1,0:T(8,128)(2,1)S(1)}, bf16[2304,256]{1,0:T(8,128)(2,1)S(1)}, u32[]{:S(2)}, u32[]{:S(2)}) collective-permute-start(bf16[2304,256]{1,0:T(8,128)(2,1)S(1)} %shard_map.129), channel_id=1, source_target_pairs={{0,8},{8,24},{24,16},{16,0},{1,9},{9,25},{25,17},{17,1},{2,10},{10... | collective-permute-start | bytes 3538952 | tf_op jit(solution)/shard_map/ppermute | solution.py:355
  81.1 3.0 %collective-permute-done.18.refs_11_ = bf16[512,2048]{1,0:T(8,128)(2,1)S(1)} collective-permute-done((bf16[512,2048]{1,0:T(8,128)(2,1)S(1)}, bf16[512,2048]{1,0:T(8,128)(2,1)S(1)}, u32[]{:S(2)}, u32[]{:S(2)}) %collective-permute-start.18) | collective-permute-done | bytes 2097184 | tf_op jit(solution)/shard_map/ppermute | solution.py:330
  84.1 3.0 %shard_map.130 = (bf16[128,2048]{1,0:T(8,128)(2,1)S(1)}, bf16[128,2048]{1,0:T(8,128)(2,1)S(1)}, bf16[256,2048]{1,0:T(8,128)(2,1)S(1)}, bf16[128,2048]{1,0:T(8,12...) custom-call(s32[1]{0:T(128)} %bitcast.1.me_ref, bf16[128,2176]{1,0:T(8,128)(2,1)S(1)} %shard_map.119.refs_0_, ...), custom_call_target="tpu_custom_call" | custom-call | flops 37748736 | bytes 139264 | tf_op jit(solution)/shard_map/pallas_call | solution.py:144
  87.1 1.6 %collective-permute-start.19 = (bf16[256,2048]{1,0:T(8,128)(2,1)S(1)}, bf16[256,2048]{1,0:T(8,128)(2,1)S(1)}, u32[]{:S(2)}, u32[]{:S(2)}) collective-permute-start(bf16[256,2048]{1,0:T(8,128)(2,1)S(1)} %get-tuple-element.100), channel_id=1, source_target_pairs={{0,2},{1,3},{2,0},{3,1},{4,6},{5,7},{6,4},{7,5},{8,10},{9,11},{10,... | collective-permute-start | bytes 3145736 | tf_op jit(solution)/shard_map/ppermute | solution.py:330
  89.8 1.3 collective-permute-start.24
  91.1 15.2 %collective-permute-done.16.refs_0_.two_ref = bf16[2304,256]{1,0:T(8,128)(2,1)S(1)} collective-permute-done((bf16[2304,256]{1,0:T(8,128)(2,1)S(1)}, bf16[2304,256]{1,0:T(8,128)(2,1)S(1)}, u32[]{:S(2)}, u32[]{:S(2)}) %collective-permute-start.16) | collective-permute-done | bytes 1179680 | tf_op jit(solution)/shard_map/ppermute | solution.py:355
  107.1 3.5 %collective-permute-start.23 = (bf16[2304,256]{1,0:T(8,128)(2,1)S(1)}, bf16[2304,256]{1,0:T(8,128)(2,1)S(1)}, u32[]{:S(2)}, u32[]{:S(2)}) collective-permute-start(bf16[2304,256]{1,0:T(8,128)(2,1)S(1)} %shard_map.132), channel_id=1, source_target_pairs={{8,16},{16,8},{9,17},{17,9},{10,18},{18,10},{11,19},{19,11},{12,20... | collective-permute-start | bytes 3538952 | tf_op jit(solution)/shard_map/ppermute | solution.py:355
  110.6 1.7 %collective-permute-done.19.refs_1_ = bf16[256,2048]{1,0:T(8,128)(2,1)S(1)} collective-permute-done((bf16[256,2048]{1,0:T(8,128)(2,1)S(1)}, bf16[256,2048]{1,0:T(8,128)(2,1)S(1)}, u32[]{:S(2)}, u32[]{:S(2)}) %collective-permute-start.19) | collective-permute-done | bytes 1048608 | tf_op jit(solution)/shard_map/ppermute | solution.py:330
  112.4 1.2 collective-permute-done.20.refs_3_.refs_4_
  115.9 10.8 %collective-permute-done.21.refs_2_ = bf16[128,2048]{1,0:T(8,128)(2,1)S(1)} collective-permute-done((bf16[128,2048]{1,0:T(8,128)(2,1)S(1)}, bf16[128,2048]{1,0:T(8,128)(2,1)S(1)}, u32[]{:S(2)}, u32[]{:S(2)}) %collective-permute-start.21) | collective-permute-done | bytes 524320 | tf_op jit(solution)/shard_map/ppermute | solution.py:330
  126.9 1.3 shard_map.135
  128.2 2.5 %collective-permute-done.24.low_ref = bf16[2304,256]{1,0:T(8,128)(2,1)S(1)} collective-permute-done((bf16[2304,256]{1,0:T(8,128)(2,1)S(1)}, bf16[2304,256]{1,0:T(8,128)(2,1)S(1)}, u32[]{:S(2)}, u32[]{:S(2)}) %collective-permute-start.24) | collective-permute-done | bytes 1179680 | tf_op jit(solution)/shard_map/ppermute | solution.py:355
  130.7 4.7 %collective-permute-done.23.up_ref = bf16[2304,256]{1,0:T(8,128)(2,1)S(1)} collective-permute-done((bf16[2304,256]{1,0:T(8,128)(2,1)S(1)}, bf16[2304,256]{1,0:T(8,128)(2,1)S(1)}, u32[]{:S(2)}, u32[]{:S(2)}) %collective-permute-start.23) | collective-permute-done | bytes 1179680 | tf_op jit(solution)/shard_map/ppermute | solution.py:355
  135.4 1.7 %shard_map.136 = (f32[512,384]{1,0:T(8,128)}, f32[512,384]{1,0:T(8,128)}, f32[96,2048]{1,0:T(8,128)}) custom-call(f32[512,768]{1,0:T(8,128)S(1)} %get-tuple-element.118.wide_ref, f32[96,2048]{1,0:T(8,128)S(1)} %get-tuple-element.119.down_ref, bf16[2304,256]{1,0:T(8,128)(2,1)S(1)} %collective-permute-done.23.up_ref, ...), custom_call_target="tpu_custom_call" | custom-call | flops 6144 | bytes 36864 | tf_op jit(solution)/shard_map/pallas_call | solution.py:283
  (49 shorter events, 17.7 us)
Async XLA Ops:
  0.6 15.1 %collective-permute-start.8 = (bf16[128,2048]{1,0:T(8,128)(2,1)}, bf16[128,2048]{1,0:T(8,128)(2,1)S(1)}, u32[]{:S(2)}, u32[]{:S(2)}) collective-permute-start(bf16[128,2048]{1,0:T(8,128)(2,1)} %refs_6_.1), channel_id=1, source_target_pairs={{0,2},{1,3},{2,0},{3,1},{4,6},{5,7},{6,4},{7,5},{8,10},{9,11},{10,... | collective-permute-start | bytes 1572872 | tf_op jit(solution)/shard_map/ppermute | solution.py:330
  1.2 15.1 %collective-permute-start.6 = (bf16[128,2048]{1,0:T(8,128)(2,1)}, bf16[128,2048]{1,0:T(8,128)(2,1)S(1)}, u32[]{:S(2)}, u32[]{:S(2)}) collective-permute-start(bf16[128,2048]{1,0:T(8,128)(2,1)} %refs_6_.1), channel_id=1, source_target_pairs={{0,4},{1,5},{2,6},{3,7},{4,0},{5,1},{6,2},{7,3},{8,12},{9,13},{10,... | collective-permute-start | bytes 1572872 | tf_op jit(solution)/shard_map/ppermute | solution.py:330
  5.0 1.0 copy-start.4
  6.3 20.5 %collective-permute-start.1 = (bf16[128,2176]{1,0:T(8,128)(2,1)S(1)}, bf16[128,2176]{1,0:T(8,128)(2,1)S(1)}, u32[]{:S(2)}, u32[]{:S(2)}) collective-permute-start(bf16[128,2176]{1,0:T(8,128)(2,1)S(1)} %shard_map.119.refs_0_), channel_id=1, source_target_pairs={{0,4},{1,5},{2,6},{3,7},{4,0},{5,1},{6,2},{7,3},{8,12},{9,13},{10,... | collective-permute-start | bytes 1671176 | tf_op jit(solution)/shard_map/ppermute | solution.py:330
  6.8 19.9 %collective-permute-start = (bf16[128,2176]{1,0:T(8,128)(2,1)S(1)}, bf16[128,2176]{1,0:T(8,128)(2,1)S(1)}, u32[]{:S(2)}, u32[]{:S(2)}) collective-permute-start(bf16[128,2176]{1,0:T(8,128)(2,1)S(1)} %shard_map.119.refs_0_), channel_id=1, source_target_pairs={{0,2},{1,3},{2,0},{3,1},{4,6},{5,7},{6,4},{7,5},{8,10},{9,11},{10,... | collective-permute-start | bytes 1671176 | tf_op jit(solution)/shard_map/ppermute | solution.py:330
  8.3 20.5 %collective-permute-start.2 = (bf16[128,2176]{1,0:T(8,128)(2,1)S(1)}, bf16[128,2176]{1,0:T(8,128)(2,1)S(1)}, u32[]{:S(2)}, u32[]{:S(2)}) collective-permute-start(bf16[128,2176]{1,0:T(8,128)(2,1)S(1)} %shard_map.119.refs_0_), channel_id=1, source_target_pairs={{0,1},{1,0},{2,3},{3,2},{4,5},{5,4},{6,7},{7,6},{8,9},{9,8},{10,11... | collective-permute-start | bytes 1671176 | tf_op jit(solution)/shard_map/ppermute | solution.py:330
  8.3 1.4 %copy-start = (bf16[1,2048,384]{2,1,0:T(8,128)(2,1)S(1)}, bf16[1,2048,384]{2,1,0:T(8,128)(2,1)}, u32[]{:S(2)}) copy-start(bf16[1,2048,384]{2,1,0:T(8,128)(2,1)} %param.11) | copy-start | bytes 4718596
  9.7 1.4 %copy-start.1 = (bf16[1,2048,384]{2,1,0:T(8,128)(2,1)S(1)}, bf16[1,2048,384]{2,1,0:T(8,128)(2,1)}, u32[]{:S(2)}) copy-start(bf16[1,2048,384]{2,1,0:T(8,128)(2,1)} %param.12) | copy-start | bytes 4718596
  11.1 1.4 %copy-start.2 = (bf16[1,384,2048]{2,1,0:T(8,128)(2,1)S(1)}, bf16[1,384,2048]{2,1,0:T(8,128)(2,1)}, u32[]{:S(2)}) copy-start(bf16[1,384,2048]{2,1,0:T(8,128)(2,1)} %param.13) | copy-start | bytes 4718596
  12.5 3.2 %copy-start.3 = (bf16[128,2048]{1,0:T(8,128)(2,1)S(1)}, bf16[128,2048]{1,0:T(8,128)(2,1)}, u32[]{:S(2)}) copy-start(bf16[128,2048]{1,0:T(8,128)(2,1)} %refs_6_.1) | copy-start | bytes 1572868
  15.7 11.6 %collective-permute-start.9 = (bf16[128,2048]{1,0:T(8,128)(2,1)S(1)}, bf16[128,2048]{1,0:T(8,128)(2,1)S(1)}, u32[]{:S(2)}, u32[]{:S(2)}) collective-permute-start(bf16[128,2048]{1,0:T(8,128)(2,1)S(1)} %copy-done.3), channel_id=1, source_target_pairs={{0,1},{1,0},{2,3},{3,2},{4,5},{5,4},{6,7},{7,6},{8,9},{9,8},{10,11... | collective-permute-start | bytes 1572872 | tf_op jit(solution)/shard_map/ppermute | solution.py:330
  16.3 12.5 %collective-permute-start.10 = (bf16[128,2048]{1,0:T(8,128)(2,1)S(1)}, bf16[128,2048]{1,0:T(8,128)(2,1)S(1)}, u32[]{:S(2)}, u32[]{:S(2)}) collective-permute-start(bf16[128,2048]{1,0:T(8,128)(2,1)S(1)} %collective-permute-done.8.refs_7_), channel_id=1, source_target_pairs={{0,1},{1,0},{2,3},{3,2},{4,5},{5,4},{6,7},{7,6},{8,9},{9,8},{10,11... | collective-permute-start | bytes 1572872 | tf_op jit(solution)/shard_map/ppermute | solution.py:330
  26.8 4.0 %collective-permute-start.4 = (bf16[128,2176]{1,0:T(8,128)(2,1)S(1)}, bf16[128,2176]{1,0:T(8,128)(2,1)S(1)}, u32[]{:S(2)}, u32[]{:S(2)}) collective-permute-start(bf16[128,2176]{1,0:T(8,128)(2,1)S(1)} %collective-permute-done.1.refs_2_), channel_id=1, source_target_pairs={{0,1},{1,0},{2,3},{3,2},{4,5},{5,4},{6,7},{7,6},{8,9},{9,8},{10,11... | collective-permute-start | bytes 1671176 | tf_op jit(solution)/shard_map/ppermute | solution.py:330
  26.8 4.0 %collective-permute-start.3 = (bf16[128,2176]{1,0:T(8,128)(2,1)S(1)}, bf16[128,2176]{1,0:T(8,128)(2,1)S(1)}, u32[]{:S(2)}, u32[]{:S(2)}) collective-permute-start(bf16[128,2176]{1,0:T(8,128)(2,1)S(1)} %collective-permute-done.refs_1_), channel_id=1, source_target_pairs={{0,1},{1,0},{2,3},{3,2},{4,5},{5,4},{6,7},{7,6},{8,9},{9,8},{10,11... | collective-permute-start | bytes 1671176 | tf_op jit(solution)/shard_map/ppermute | solution.py:330
  27.3 15.9 %collective-permute-start.5 = (bf16[128,2176]{1,0:T(8,128)(2,1)S(1)}, bf16[128,2176]{1,0:T(8,128)(2,1)S(1)}, u32[]{:S(2)}, u32[]{:S(2)}) collective-permute-start(bf16[128,2176]{1,0:T(8,128)(2,1)S(1)} %collective-permute-done.refs_1_), channel_id=1, source_target_pairs={{0,4},{1,5},{2,6},{3,7},{4,0},{5,1},{6,2},{7,3},{8,12},{9,13},{10,... | collective-permute-start | bytes 1671176 | tf_op jit(solution)/shard_map/ppermute | solution.py:330
  28.8 1.9 %collective-permute-start.11 = (bf16[128,2048]{1,0:T(8,128)(2,1)S(1)}, bf16[128,2048]{1,0:T(8,128)(2,1)S(1)}, u32[]{:S(2)}, u32[]{:S(2)}) collective-permute-start(bf16[128,2048]{1,0:T(8,128)(2,1)S(1)} %collective-permute-done.6.refs_8_), channel_id=1, source_target_pairs={{0,1},{1,0},{2,3},{3,2},{4,5},{5,4},{6,7},{7,6},{8,9},{9,8},{10,11... | collective-permute-start | bytes 1572872 | tf_op jit(solution)/shard_map/ppermute | solution.py:330
  28.8 14.3 %collective-permute-start.7 = (bf16[128,2048]{1,0:T(8,128)(2,1)S(1)}, bf16[128,2048]{1,0:T(8,128)(2,1)S(1)}, u32[]{:S(2)}, u32[]{:S(2)}) collective-permute-start(bf16[128,2048]{1,0:T(8,128)(2,1)S(1)} %collective-permute-done.6.refs_8_), channel_id=1, source_target_pairs={{0,2},{1,3},{2,0},{3,1},{4,6},{5,7},{6,4},{7,5},{8,10},{9,11},{10,... | collective-permute-start | bytes 1572872 | tf_op jit(solution)/shard_map/ppermute | solution.py:330
  43.2 2.7 %collective-permute-start.12 = (bf16[128,2176]{1,0:T(8,128)(2,1)S(1)}, bf16[128,2176]{1,0:T(8,128)(2,1)S(1)}, u32[]{:S(2)}, u32[]{:S(2)}) collective-permute-start(bf16[128,2176]{1,0:T(8,128)(2,1)S(1)} %collective-permute-done.5.refs_0_.refs_6_.refs_3_), channel_id=1, source_target_pairs={{0,1},{1,0},{2,3},{3,2},{4,5},{5,4},{6,7},{7,6},{8,9},{9,8},{10,11... | collective-permute-start | bytes 1671176 | tf_op jit(solution)/shard_map/ppermute | solution.py:330
  43.2 2.7 %collective-permute-start.13 = (bf16[128,2048]{1,0:T(8,128)(2,1)S(1)}, bf16[128,2048]{1,0:T(8,128)(2,1)S(1)}, u32[]{:S(2)}, u32[]{:S(2)}) collective-permute-start(bf16[128,2048]{1,0:T(8,128)(2,1)S(1)} %collective-permute-done.7.refs_1_), channel_id=1, source_target_pairs={{0,1},{1,0},{2,3},{3,2},{4,5},{5,4},{6,7},{7,6},{8,9},{9,8},{10,11... | collective-permute-start | bytes 1572872 | tf_op jit(solution)/shard_map/ppermute | solution.py:330
  47.9 28.1 %collective-permute-start.14 = (bf16[512,768]{1,0:T(8,128)(2,1)S(1)}, bf16[512,768]{1,0:T(8,128)(2,1)S(1)}, u32[]{:S(2)}, u32[]{:S(2)}) collective-permute-start(bf16[512,768]{1,0:T(8,128)(2,1)S(1)} %shard_map.125), channel_id=1, source_target_pairs={{0,8},{8,0},{16,24},{24,16},{1,9},{9,1},{17,25},{25,17},{2,10},{10... | collective-permute-start | bytes 2359304 | tf_op jit(solution)/shard_map/ppermute | solution.py:355
  50.8 25.1 %collective-permute-start.15 = (bf16[96,2048]{1,0:T(8,128)(2,1)S(1)}, bf16[96,2048]{1,0:T(8,128)(2,1)S(1)}, u32[]{:S(2)}, u32[]{:S(2)}) collective-permute-start(bf16[96,2048]{1,0:T(8,128)(2,1)S(1)} %get-tuple-element.83), channel_id=1, source_target_pairs={{0,8},{8,0},{16,24},{24,16},{1,9},{9,1},{17,25},{25,17},{2,10},{10... | collective-permute-start | bytes 1179656 | tf_op jit(solution)/shard_map/ppermute | solution.py:355
  76.8 4.2 %collective-permute-start.17 = (bf16[512,2048]{1,0:T(8,128)(2,1)S(1)}, bf16[512,2048]{1,0:T(8,128)(2,1)S(1)}, u32[]{:S(2)}, u32[]{:S(2)}) collective-permute-start(bf16[512,2048]{1,0:T(8,128)(2,1)S(1)} %get-tuple-element.96), channel_id=1, source_target_pairs={{0,1},{1,0},{2,3},{3,2},{4,5},{5,4},{6,7},{7,6},{8,9},{9,8},{10,11... | collective-permute-start | bytes 6291464 | tf_op jit(solution)/shard_map/ppermute | solution.py:330
  76.9 7.1 %collective-permute-start.18 = (bf16[512,2048]{1,0:T(8,128)(2,1)S(1)}, bf16[512,2048]{1,0:T(8,128)(2,1)S(1)}, u32[]{:S(2)}, u32[]{:S(2)}) collective-permute-start(bf16[512,2048]{1,0:T(8,128)(2,1)S(1)} %get-tuple-element.97), channel_id=1, source_target_pairs={{0,1},{1,0},{2,3},{3,2},{4,5},{5,4},{6,7},{7,6},{8,9},{9,8},{10,11... | collective-permute-start | bytes 6291464 | tf_op jit(solution)/shard_map/ppermute | solution.py:330
  77.4 28.8 %collective-permute-start.16 = (bf16[2304,256]{1,0:T(8,128)(2,1)S(1)}, bf16[2304,256]{1,0:T(8,128)(2,1)S(1)}, u32[]{:S(2)}, u32[]{:S(2)}) collective-permute-start(bf16[2304,256]{1,0:T(8,128)(2,1)S(1)} %shard_map.129), channel_id=1, source_target_pairs={{0,8},{8,24},{24,16},{16,0},{1,9},{9,25},{25,17},{17,1},{2,10},{10... | collective-permute-start | bytes 3538952 | tf_op jit(solution)/shard_map/ppermute | solution.py:355
  87.1 25.3 %collective-permute-start.19 = (bf16[256,2048]{1,0:T(8,128)(2,1)S(1)}, bf16[256,2048]{1,0:T(8,128)(2,1)S(1)}, u32[]{:S(2)}, u32[]{:S(2)}) collective-permute-start(bf16[256,2048]{1,0:T(8,128)(2,1)S(1)} %get-tuple-element.100), channel_id=1, source_target_pairs={{0,2},{1,3},{2,0},{3,1},{4,6},{5,7},{6,4},{7,5},{8,10},{9,11},{10,... | collective-permute-start | bytes 3145736 | tf_op jit(solution)/shard_map/ppermute | solution.py:330
  88.6 24.9 %collective-permute-start.20 = (bf16[256,2048]{1,0:T(8,128)(2,1)S(1)}, bf16[256,2048]{1,0:T(8,128)(2,1)S(1)}, u32[]{:S(2)}, u32[]{:S(2)}) collective-permute-start(bf16[256,2048]{1,0:T(8,128)(2,1)S(1)} %get-tuple-element.103), channel_id=1, source_target_pairs={{0,4},{1,5},{2,6},{3,7},{4,0},{5,1},{6,2},{7,3},{8,12},{9,13},{10,... | collective-permute-start | bytes 3145736 | tf_op jit(solution)/shard_map/ppermute | solution.py:330
  89.8 40.9 %collective-permute-start.24 = (bf16[2304,256]{1,0:T(8,128)(2,1)S(1)}, bf16[2304,256]{1,0:T(8,128)(2,1)S(1)}, u32[]{:S(2)}, u32[]{:S(2)}) collective-permute-start(bf16[2304,256]{1,0:T(8,128)(2,1)S(1)} %shard_map.131), channel_id=1, source_target_pairs={{0,8},{24,16},{1,9},{25,17},{2,10},{26,18},{3,11},{27,19},{4,12},{... | collective-permute-start | bytes 3538952 | tf_op jit(solution)/shard_map/ppermute | solution.py:355
  107.1 28.2 %collective-permute-start.23 = (bf16[2304,256]{1,0:T(8,128)(2,1)S(1)}, bf16[2304,256]{1,0:T(8,128)(2,1)S(1)}, u32[]{:S(2)}, u32[]{:S(2)}) collective-permute-start(bf16[2304,256]{1,0:T(8,128)(2,1)S(1)} %shard_map.132), channel_id=1, source_target_pairs={{8,16},{16,8},{9,17},{17,9},{10,18},{18,10},{11,19},{19,11},{12,20... | collective-permute-start | bytes 3538952 | tf_op jit(solution)/shard_map/ppermute | solution.py:355
  113.8 12.9 %collective-permute-start.21 = (bf16[128,2048]{1,0:T(8,128)(2,1)S(1)}, bf16[128,2048]{1,0:T(8,128)(2,1)S(1)}, u32[]{:S(2)}, u32[]{:S(2)}) collective-permute-start(bf16[128,2048]{1,0:T(8,128)(2,1)S(1)} %get-tuple-element.109), channel_id=1, source_target_pairs={{0,4},{1,5},{2,6},{3,7},{4,0},{5,1},{6,2},{7,3},{8,12},{9,13},{10,... | collective-permute-start | bytes 1572872 | tf_op jit(solution)/shard_map/ppermute | solution.py:330
  114.4 12.5 %collective-permute-start.22 = (bf16[128,2048]{1,0:T(8,128)(2,1)S(1)}, bf16[128,2048]{1,0:T(8,128)(2,1)S(1)}, u32[]{:S(2)}, u32[]{:S(2)}) collective-permute-start(bf16[128,2048]{1,0:T(8,128)(2,1)S(1)} %get-tuple-element.110), channel_id=1, source_target_pairs={{0,2},{1,3},{2,0},{3,1},{4,6},{5,7},{6,4},{7,5},{8,10},{9,11},{10,... | collective-permute-start | bytes 1572872 | tf_op jit(solution)/shard_map/ppermute | solution.py:330

commit v2 on v1

--- a/solution.py
+++ b/solution.py
@@ -226,13 +226,22 @@
 def join_kernel(order_ref, wide_own, down_own, *refs):
     came, out_ref = refs[:-1], refs[-1]
     owns = wide_own, down_own
-    for number, rows, part in pieces(wide_own.shape, down_own.shape):
-        own = owns[number][:, part]
-        if came:
+    parts = list(pieces(wide_own.shape, down_own.shape))
+
+    def own_terms():
+        for number, rows, part in parts:
+            out_ref[rows, :] = owns[number][:, part]
+
+    def with_arrivals():
+        for number, rows, part in parts:
             other = came[0][rows, :] if len(came) == 1 else came[number][:, part]
-            other = jnp.where(order_ref[4] == 1, other.astype(F32), 0.0)
-            own = (own.astype(F32) + other).astype(BF16)
-        out_ref[rows, :] = own
+            out_ref[rows, :] = owns[number][:, part] + other
+
+    if came:
+        pl.when(order_ref[4] == 0)(own_terms)
+        pl.when(order_ref[4] == 1)(with_arrivals)
+    else:
+        own_terms()
 
 
 def join(order, wide_own, down_own, *came):

time: 138 us -> 138 us (level)
  no operation moved by 1% of the time
where the time goes in v2:
time: 138 us; the launch traced here: 137 us
  waiting for transfers between devices  79.4 us (58%)
  Pallas kernels  27.4 us (20%)
  starting transfers between devices  21.5 us (16%)
  local copies, waits for them, and re-layouts  7.54 us (5%)
    ppermute x20, waiting for transfers between devices, flip(): return lax.ppermute(array, 'expert', [(i, i ^ bit) for i in range(group)])  40.1 us
    ppermute x5, waiting for transfers between devices, move(): return lax.ppermute(array, 'dp', pairs) if line else array  39.3 us
    ppermute x20, starting transfers between devices, flip(): return lax.ppermute(array, 'expert', [(i, i ^ bit) for i in range(group)])  12 us
    ppermute x5, starting transfers between devices, move(): return lax.ppermute(array, 'dp', pairs) if line else array  9.47 us
    unnamed x12, local copies, waits for them, and re-layouts  6.86 us
    pallas_call x3, Pallas kernels, hidden(): pl.pallas_call(functools.partial(hidden_kernel, blocks), out_shape=outs,...  6.56 us
    pallas_call x2, Pallas kernels, rows_out(): pl.pallas_call(functools.partial(rows_kernel, blocks, groups, part, place...  6.09 us
    pallas_call x3, Pallas kernels, wide_grads(): pl.pallas_call(functools.partial(wide_grad_kernel, blocks, len(hids), fir...  5.56 us
  transfers between devices with their start and end apart: 25, of which 16 were waited for; matrix products, arithmetic and copies ran while one was open for 2% of the time, Pallas kernels for 17%

profile of v2, /device:TPU:10, one launch (start us, length us, event | category | flops | bytes accessed | tf_op | source)
XLA Modules:
  0.0 136.6 jit_solution(13920919862897031590)
XLA Ops:
  1.2 1.5 %collective-permute-start.6 = (bf16[128,2048]{1,0:T(8,128)(2,1)}, bf16[128,2048]{1,0:T(8,128)(2,1)S(1)}, u32[]{:S(2)}, u32[]{:S(2)}) collective-permute-start(bf16[128,2048]{1,0:T(8,128)(2,1)} %refs_6_.1), channel_id=1, source_target_pairs={{0,4},{1,5},{2,6},{3,7},{4,0},{5,1},{6,2},{7,3},{8,12},{9,13},{10,... | collective-permute-start | bytes 1572872 | tf_op jit(solution)/shard_map/ppermute | solution.py:339
  6.8 1.5 %collective-permute-start = (bf16[128,2176]{1,0:T(8,128)(2,1)S(1)}, bf16[128,2176]{1,0:T(8,128)(2,1)S(1)}, u32[]{:S(2)}, u32[]{:S(2)}) collective-permute-start(bf16[128,2176]{1,0:T(8,128)(2,1)S(1)} %shard_map.119.refs_0_), channel_id=1, source_target_pairs={{0,2},{1,3},{2,0},{3,1},{4,6},{5,7},{6,4},{7,5},{8,10},{9,11},{10,... | collective-permute-start | bytes 1671176 | tf_op jit(solution)/shard_map/ppermute | solution.py:339
  8.3 1.4 %copy-done = bf16[1,2048,384]{2,1,0:T(8,128)(2,1)S(1)} copy-done((bf16[1,2048,384]{2,1,0:T(8,128)(2,1)S(1)}, bf16[1,2048,384]{2,1,0:T(8,128)(2,1)}, u32[]{:S(2)}) %copy-start) | copy-done | bytes 1572888
  9.7 1.4 %copy-done.1 = bf16[1,2048,384]{2,1,0:T(8,128)(2,1)S(1)} copy-done((bf16[1,2048,384]{2,1,0:T(8,128)(2,1)S(1)}, bf16[1,2048,384]{2,1,0:T(8,128)(2,1)}, u32[]{:S(2)}) %copy-start.1) | copy-done | bytes 1572888
  11.1 1.4 %copy-done.2 = bf16[1,384,2048]{2,1,0:T(8,128)(2,1)S(1)} copy-done((bf16[1,384,2048]{2,1,0:T(8,128)(2,1)S(1)}, bf16[1,384,2048]{2,1,0:T(8,128)(2,1)}, u32[]{:S(2)}) %copy-start.2) | copy-done | bytes 1572888
  12.9 2.8 %collective-permute-done.8.refs_7_ = bf16[128,2048]{1,0:T(8,128)(2,1)S(1)} collective-permute-done((bf16[128,2048]{1,0:T(8,128)(2,1)}, bf16[128,2048]{1,0:T(8,128)(2,1)S(1)}, u32[]{:S(2)}, u32[]{:S(2)}) %collective-permute-start.8) | collective-permute-done | bytes 524320 | tf_op jit(solution)/shard_map/ppermute | solution.py:339
  16.3 10.5 %collective-permute-done.1.refs_2_ = bf16[128,2176]{1,0:T(8,128)(2,1)S(1)} collective-permute-done((bf16[128,2176]{1,0:T(8,128)(2,1)S(1)}, bf16[128,2176]{1,0:T(8,128)(2,1)S(1)}, u32[]{:S(2)}, u32[]{:S(2)}) %collective-permute-start.1) | collective-permute-done | bytes 557088 | tf_op jit(solution)/shard_map/ppermute | solution.py:339
  27.3 1.5 %collective-permute-start.5 = (bf16[128,2176]{1,0:T(8,128)(2,1)S(1)}, bf16[128,2176]{1,0:T(8,128)(2,1)S(1)}, u32[]{:S(2)}, u32[]{:S(2)}) collective-permute-start(bf16[128,2176]{1,0:T(8,128)(2,1)S(1)} %collective-permute-done.refs_1_), channel_id=1, source_target_pairs={{0,4},{1,5},{2,6},{3,7},{4,0},{5,1},{6,2},{7,3},{8,12},{9,13},{10,... | collective-permute-start | bytes 1671176 | tf_op jit(solution)/shard_map/ppermute | solution.py:339
  28.8 1.6 %collective-permute-start.7 = (bf16[128,2048]{1,0:T(8,128)(2,1)S(1)}, bf16[128,2048]{1,0:T(8,128)(2,1)S(1)}, u32[]{:S(2)}, u32[]{:S(2)}) collective-permute-start(bf16[128,2048]{1,0:T(8,128)(2,1)S(1)} %collective-permute-done.6.refs_8_), channel_id=1, source_target_pairs={{0,2},{1,3},{2,0},{3,1},{4,6},{5,7},{6,4},{7,5},{8,10},{9,11},{10,... | collective-permute-start | bytes 1572872 | tf_op jit(solution)/shard_map/ppermute | solution.py:339
  30.7 4.5 %shard_map.121 = (bf16[768,384]{1,0:T(8,128)(2,1)S(1)}, bf16[768,768]{1,0:T(8,128)(2,1)S(1)}, bf16[768,2048]{1,0:T(8,128)(2,1)S(1)}) custom-call(s32[1]{0:T(128)} %bitcast.1.me_ref, bf16[128,2176]{1,0:T(8,128)(2,1)S(1)} %shard_map.119.refs_0_, bf16[128,2176]{1,0:T(8,128)(2,1)S(1)} %collective-permute-done.refs_1_, ...), custom_call_target="tpu_custom_call" | custom-call | flops 56623104 | bytes 251904 | tf_op jit(solution)/shard_map/pallas_call | solution.py:95
  35.2 1.4 %shard_map.122.refs_4_ = f32[512,768]{1,0:T(8,128)S(1)} custom-call(s32[5]{0:T(128)S(1)} %dynamic-slice_bitcast_fusion.order_ref, bf16[128,2176]{1,0:T(8,128)(2,1)S(1)} %shard_map.119.refs_0_, bf16[128,2176]{1,0:T(8,128)(2,1)S(1)} %collective-permute-done.refs_1_, bf16[128,2176]{1,0:T(8,128)(2,1)S(1)} %collective-permute-done.1.refs_2_, ...), custom_call_target="tpu_custom_call" | custom-call | flops 9437184 | bytes 43008 | tf_op jit(solution)/shard_map/pallas_call | solution.py:175
  36.6 6.6 %collective-permute-done.7.refs_1_ = bf16[128,2048]{1,0:T(8,128)(2,1)S(1)} collective-permute-done((bf16[128,2048]{1,0:T(8,128)(2,1)S(1)}, bf16[128,2048]{1,0:T(8,128)(2,1)S(1)}, u32[]{:S(2)}, u32[]{:S(2)}) %collective-permute-start.7) | collective-permute-done | bytes 524320 | tf_op jit(solution)/shard_map/ppermute | solution.py:339
  44.7 1.2 collective-permute-done.13.refs_1_
  48.4 2.4 %shard_map.126 = (bf16[96,2048]{1,0:T(8,128)(2,1)S(1)}, bf16[96,2048]{1,0:T(8,128)(2,1)S(1)}, bf16[96,2048]{1,0:T(8,128)(2,1)S(1)}, bf16[96,2048]{1,0:T(8,128)(2,1)S(1)}) custom-call(s32[5]{0:T(128)S(1)} %dynamic-slice_bitcast_fusion.order_ref, bf16[768,384]{1,0:T(8,128)(2,1)S(1)} %get-tuple-element.90.refs_0_.refs_4_, ...), custom_call_target="tpu_custom_call" | custom-call | flops 25165824 | bytes 77824 | tf_op jit(solution)/shard_map/pallas_call | solution.py:204
  50.8 1.6 %collective-permute-start.15 = (bf16[96,2048]{1,0:T(8,128)(2,1)S(1)}, bf16[96,2048]{1,0:T(8,128)(2,1)S(1)}, u32[]{:S(2)}, u32[]{:S(2)}) collective-permute-start(bf16[96,2048]{1,0:T(8,128)(2,1)S(1)} %get-tuple-element.83), channel_id=1, source_target_pairs={{0,8},{8,0},{16,24},{24,16},{1,9},{9,1},{17,25},{25,17},{2,10},{10... | collective-permute-start | bytes 1179656 | tf_op jit(solution)/shard_map/ppermute | solution.py:364
  52.5 3.2 %shard_map.127 = (bf16[512,768]{1,0:T(8,128)(2,1)S(1)}, bf16[512,768]{1,0:T(8,128)(2,1)S(1)}, bf16[512,768]{1,0:T(8,128)(2,1)S(1)}) custom-call(s32[5]{0:T(128)S(1)} %dynamic-slice_bitcast_fusion.order_ref, bf16[128,2176]{1,0:T(8,128)(2,1)S(1)} %shard_map.119.refs_0_, bf16[128,2176]{1,0:T(8,128)(2,1)S(1)} %collective-permute-done.refs_1_, ...), custom_call_target="tpu_custom_call" | custom-call | flops 37748736 | bytes 61440 | tf_op jit(solution)/shard_map/pallas_call | solution.py:175
  55.7 3.1 %shard_map.128 = (bf16[512,2048]{1,0:T(8,128)(2,1)S(1)}, bf16[512,2048]{1,0:T(8,128)(2,1)S(1)}) custom-call(s32[1]{0:T(128)} %bitcast.1.me_ref, bf16[128,2176]{1,0:T(8,128)(2,1)S(1)} %collective-permute-done.2.refs_3_.refs_0_, bf16[128,2176]{1,0:T(8,128)(2,1)S(1)} %collective-permute-done.3.refs_4_.refs_1_, ...), custom_call_target="tpu_custom_call" | custom-call | flops 37748736 | bytes 139264 | tf_op jit(solution)/shard_map/pallas_call | solution.py:144
  58.8 17.2 %collective-permute-done.15.refs_1_.down_one = bf16[96,2048]{1,0:T(8,128)(2,1)S(1)} collective-permute-done((bf16[96,2048]{1,0:T(8,128)(2,1)S(1)}, bf16[96,2048]{1,0:T(8,128)(2,1)S(1)}, u32[]{:S(2)}, u32[]{:S(2)}) %collective-permute-start.15) | collective-permute-done | bytes 393248 | tf_op jit(solution)/shard_map/ppermute | solution.py:364
  77.2 2.5 %collective-permute-start.16 = (bf16[2304,256]{1,0:T(8,128)(2,1)S(1)}, bf16[2304,256]{1,0:T(8,128)(2,1)S(1)}, u32[]{:S(2)}, u32[]{:S(2)}) collective-permute-start(bf16[2304,256]{1,0:T(8,128)(2,1)S(1)} %shard_map.129), channel_id=1, source_target_pairs={{0,8},{8,24},{24,16},{16,0},{1,9},{9,25},{25,17},{17,1},{2,10},{10... | collective-permute-start | bytes 3538952 | tf_op jit(solution)/shard_map/ppermute | solution.py:364
  80.9 3.0 %collective-permute-done.18.refs_11_ = bf16[512,2048]{1,0:T(8,128)(2,1)S(1)} collective-permute-done((bf16[512,2048]{1,0:T(8,128)(2,1)S(1)}, bf16[512,2048]{1,0:T(8,128)(2,1)S(1)}, u32[]{:S(2)}, u32[]{:S(2)}) %collective-permute-start.18) | collective-permute-done | bytes 2097184 | tf_op jit(solution)/shard_map/ppermute | solution.py:339
  83.9 3.0 %shard_map.130 = (bf16[128,2048]{1,0:T(8,128)(2,1)S(1)}, bf16[128,2048]{1,0:T(8,128)(2,1)S(1)}, bf16[256,2048]{1,0:T(8,128)(2,1)S(1)}, bf16[128,2048]{1,0:T(8,12...) custom-call(s32[1]{0:T(128)} %bitcast.1.me_ref, bf16[128,2176]{1,0:T(8,128)(2,1)S(1)} %shard_map.119.refs_0_, ...), custom_call_target="tpu_custom_call" | custom-call | flops 37748736 | bytes 139264 | tf_op jit(solution)/shard_map/pallas_call | solution.py:144
  86.9 1.6 %collective-permute-start.19 = (bf16[256,2048]{1,0:T(8,128)(2,1)S(1)}, bf16[256,2048]{1,0:T(8,128)(2,1)S(1)}, u32[]{:S(2)}, u32[]{:S(2)}) collective-permute-start(bf16[256,2048]{1,0:T(8,128)(2,1)S(1)} %get-tuple-element.100), channel_id=1, source_target_pairs={{0,2},{1,3},{2,0},{3,1},{4,6},{5,7},{6,4},{7,5},{8,10},{9,11},{10,... | collective-permute-start | bytes 3145736 | tf_op jit(solution)/shard_map/ppermute | solution.py:339
  89.6 1.3 collective-permute-start.24
  90.9 15.2 %collective-permute-done.16.refs_0_.two_ref = bf16[2304,256]{1,0:T(8,128)(2,1)S(1)} collective-permute-done((bf16[2304,256]{1,0:T(8,128)(2,1)S(1)}, bf16[2304,256]{1,0:T(8,128)(2,1)S(1)}, u32[]{:S(2)}, u32[]{:S(2)}) %collective-permute-start.16) | collective-permute-done | bytes 1179680 | tf_op jit(solution)/shard_map/ppermute | solution.py:364
  106.7 3.5 %collective-permute-start.23 = (bf16[2304,256]{1,0:T(8,128)(2,1)S(1)}, bf16[2304,256]{1,0:T(8,128)(2,1)S(1)}, u32[]{:S(2)}, u32[]{:S(2)}) collective-permute-start(bf16[2304,256]{1,0:T(8,128)(2,1)S(1)} %shard_map.132), channel_id=1, source_target_pairs={{8,16},{16,8},{9,17},{17,9},{10,18},{18,10},{11,19},{19,11},{12,20... | collective-permute-start | bytes 3538952 | tf_op jit(solution)/shard_map/ppermute | solution.py:364
  110.2 1.9 %collective-permute-done.19.refs_1_ = bf16[256,2048]{1,0:T(8,128)(2,1)S(1)} collective-permute-done((bf16[256,2048]{1,0:T(8,128)(2,1)S(1)}, bf16[256,2048]{1,0:T(8,128)(2,1)S(1)}, u32[]{:S(2)}, u32[]{:S(2)}) %collective-permute-start.19) | collective-permute-done | bytes 1048608 | tf_op jit(solution)/shard_map/ppermute | solution.py:339
  112.1 1.2 collective-permute-done.20.refs_3_.refs_4_
  115.7 10.8 %collective-permute-done.21.refs_2_ = bf16[128,2048]{1,0:T(8,128)(2,1)S(1)} collective-permute-done((bf16[128,2048]{1,0:T(8,128)(2,1)S(1)}, bf16[128,2048]{1,0:T(8,128)(2,1)S(1)}, u32[]{:S(2)}, u32[]{:S(2)}) %collective-permute-start.21) | collective-permute-done | bytes 524320 | tf_op jit(solution)/shard_map/ppermute | solution.py:339
  126.7 1.3 shard_map.135
  128.0 2.5 %collective-permute-done.24.low_ref = bf16[2304,256]{1,0:T(8,128)(2,1)S(1)} collective-permute-done((bf16[2304,256]{1,0:T(8,128)(2,1)S(1)}, bf16[2304,256]{1,0:T(8,128)(2,1)S(1)}, u32[]{:S(2)}, u32[]{:S(2)}) %collective-permute-start.24) | collective-permute-done | bytes 1179680 | tf_op jit(solution)/shard_map/ppermute | solution.py:364
  130.4 4.5 %collective-permute-done.23.up_ref = bf16[2304,256]{1,0:T(8,128)(2,1)S(1)} collective-permute-done((bf16[2304,256]{1,0:T(8,128)(2,1)S(1)}, bf16[2304,256]{1,0:T(8,128)(2,1)S(1)}, u32[]{:S(2)}, u32[]{:S(2)}) %collective-permute-start.23) | collective-permute-done | bytes 1179680 | tf_op jit(solution)/shard_map/ppermute | solution.py:364
  134.9 1.7 %shard_map.136 = (f32[512,384]{1,0:T(8,128)}, f32[512,384]{1,0:T(8,128)}, f32[96,2048]{1,0:T(8,128)}) custom-call(f32[512,768]{1,0:T(8,128)S(1)} %get-tuple-element.118.wide_ref, f32[96,2048]{1,0:T(8,128)S(1)} %get-tuple-element.119.down_ref, bf16[2304,256]{1,0:T(8,128)(2,1)S(1)} %collective-permute-done.23.up_ref, ...), custom_call_target="tpu_custom_call" | custom-call | flops 6144 | bytes 36864 | tf_op jit(solution)/shard_map/pallas_call | solution.py:292
  (49 shorter events, 17.3 us)
Async XLA Ops:
  0.6 15.1 %collective-permute-start.8 = (bf16[128,2048]{1,0:T(8,128)(2,1)}, bf16[128,2048]{1,0:T(8,128)(2,1)S(1)}, u32[]{:S(2)}, u32[]{:S(2)}) collective-permute-start(bf16[128,2048]{1,0:T(8,128)(2,1)} %refs_6_.1), channel_id=1, source_target_pairs={{0,2},{1,3},{2,0},{3,1},{4,6},{5,7},{6,4},{7,5},{8,10},{9,11},{10,... | collective-permute-start | bytes 1572872 | tf_op jit(solution)/shard_map/ppermute | solution.py:339
  1.2 15.1 %collective-permute-start.6 = (bf16[128,2048]{1,0:T(8,128)(2,1)}, bf16[128,2048]{1,0:T(8,128)(2,1)S(1)}, u32[]{:S(2)}, u32[]{:S(2)}) collective-permute-start(bf16[128,2048]{1,0:T(8,128)(2,1)} %refs_6_.1), channel_id=1, source_target_pairs={{0,4},{1,5},{2,6},{3,7},{4,0},{5,1},{6,2},{7,3},{8,12},{9,13},{10,... | collective-permute-start | bytes 1572872 | tf_op jit(solution)/shard_map/ppermute | solution.py:339
  5.0 1.0 copy-start.4
  6.3 20.5 %collective-permute-start.1 = (bf16[128,2176]{1,0:T(8,128)(2,1)S(1)}, bf16[128,2176]{1,0:T(8,128)(2,1)S(1)}, u32[]{:S(2)}, u32[]{:S(2)}) collective-permute-start(bf16[128,2176]{1,0:T(8,128)(2,1)S(1)} %shard_map.119.refs_0_), channel_id=1, source_target_pairs={{0,4},{1,5},{2,6},{3,7},{4,0},{5,1},{6,2},{7,3},{8,12},{9,13},{10,... | collective-permute-start | bytes 1671176 | tf_op jit(solution)/shard_map/ppermute | solution.py:339
  6.8 19.9 %collective-permute-start = (bf16[128,2176]{1,0:T(8,128)(2,1)S(1)}, bf16[128,2176]{1,0:T(8,128)(2,1)S(1)}, u32[]{:S(2)}, u32[]{:S(2)}) collective-permute-start(bf16[128,2176]{1,0:T(8,128)(2,1)S(1)} %shard_map.119.refs_0_), channel_id=1, source_target_pairs={{0,2},{1,3},{2,0},{3,1},{4,6},{5,7},{6,4},{7,5},{8,10},{9,11},{10,... | collective-permute-start | bytes 1671176 | tf_op jit(solution)/shard_map/ppermute | solution.py:339
  8.3 20.5 %collective-permute-start.2 = (bf16[128,2176]{1,0:T(8,128)(2,1)S(1)}, bf16[128,2176]{1,0:T(8,128)(2,1)S(1)}, u32[]{:S(2)}, u32[]{:S(2)}) collective-permute-start(bf16[128,2176]{1,0:T(8,128)(2,1)S(1)} %shard_map.119.refs_0_), channel_id=1, source_target_pairs={{0,1},{1,0},{2,3},{3,2},{4,5},{5,4},{6,7},{7,6},{8,9},{9,8},{10,11... | collective-permute-start | bytes 1671176 | tf_op jit(solution)/shard_map/ppermute | solution.py:339
  8.3 1.4 %copy-start = (bf16[1,2048,384]{2,1,0:T(8,128)(2,1)S(1)}, bf16[1,2048,384]{2,1,0:T(8,128)(2,1)}, u32[]{:S(2)}) copy-start(bf16[1,2048,384]{2,1,0:T(8,128)(2,1)} %param.11) | copy-start | bytes 4718596
  9.7 1.4 %copy-start.1 = (bf16[1,2048,384]{2,1,0:T(8,128)(2,1)S(1)}, bf16[1,2048,384]{2,1,0:T(8,128)(2,1)}, u32[]{:S(2)}) copy-start(bf16[1,2048,384]{2,1,0:T(8,128)(2,1)} %param.12) | copy-start | bytes 4718596
  11.1 1.4 %copy-start.2 = (bf16[1,384,2048]{2,1,0:T(8,128)(2,1)S(1)}, bf16[1,384,2048]{2,1,0:T(8,128)(2,1)}, u32[]{:S(2)}) copy-start(bf16[1,384,2048]{2,1,0:T(8,128)(2,1)} %param.13) | copy-start | bytes 4718596
  12.5 3.2 %copy-start.3 = (bf16[128,2048]{1,0:T(8,128)(2,1)S(1)}, bf16[128,2048]{1,0:T(8,128)(2,1)}, u32[]{:S(2)}) copy-start(bf16[128,2048]{1,0:T(8,128)(2,1)} %refs_6_.1) | copy-start | bytes 1572868
  15.7 11.6 %collective-permute-start.9 = (bf16[128,2048]{1,0:T(8,128)(2,1)S(1)}, bf16[128,2048]{1,0:T(8,128)(2,1)S(1)}, u32[]{:S(2)}, u32[]{:S(2)}) collective-permute-start(bf16[128,2048]{1,0:T(8,128)(2,1)S(1)} %copy-done.3), channel_id=1, source_target_pairs={{0,1},{1,0},{2,3},{3,2},{4,5},{5,4},{6,7},{7,6},{8,9},{9,8},{10,11... | collective-permute-start | bytes 1572872 | tf_op jit(solution)/shard_map/ppermute | solution.py:339
  16.3 12.5 %collective-permute-start.10 = (bf16[128,2048]{1,0:T(8,128)(2,1)S(1)}, bf16[128,2048]{1,0:T(8,128)(2,1)S(1)}, u32[]{:S(2)}, u32[]{:S(2)}) collective-permute-start(bf16[128,2048]{1,0:T(8,128)(2,1)S(1)} %collective-permute-done.8.refs_7_), channel_id=1, source_target_pairs={{0,1},{1,0},{2,3},{3,2},{4,5},{5,4},{6,7},{7,6},{8,9},{9,8},{10,11... | collective-permute-start | bytes 1572872 | tf_op jit(solution)/shard_map/ppermute | solution.py:339
  26.8 4.0 %collective-permute-start.4 = (bf16[128,2176]{1,0:T(8,128)(2,1)S(1)}, bf16[128,2176]{1,0:T(8,128)(2,1)S(1)}, u32[]{:S(2)}, u32[]{:S(2)}) collective-permute-start(bf16[128,2176]{1,0:T(8,128)(2,1)S(1)} %collective-permute-done.1.refs_2_), channel_id=1, source_target_pairs={{0,1},{1,0},{2,3},{3,2},{4,5},{5,4},{6,7},{7,6},{8,9},{9,8},{10,11... | collective-permute-start | bytes 1671176 | tf_op jit(solution)/shard_map/ppermute | solution.py:339
  26.8 4.0 %collective-permute-start.3 = (bf16[128,2176]{1,0:T(8,128)(2,1)S(1)}, bf16[128,2176]{1,0:T(8,128)(2,1)S(1)}, u32[]{:S(2)}, u32[]{:S(2)}) collective-permute-start(bf16[128,2176]{1,0:T(8,128)(2,1)S(1)} %collective-permute-done.refs_1_), channel_id=1, source_target_pairs={{0,1},{1,0},{2,3},{3,2},{4,5},{5,4},{6,7},{7,6},{8,9},{9,8},{10,11... | collective-permute-start | bytes 1671176 | tf_op jit(solution)/shard_map/ppermute | solution.py:339
  27.3 15.9 %collective-permute-start.5 = (bf16[128,2176]{1,0:T(8,128)(2,1)S(1)}, bf16[128,2176]{1,0:T(8,128)(2,1)S(1)}, u32[]{:S(2)}, u32[]{:S(2)}) collective-permute-start(bf16[128,2176]{1,0:T(8,128)(2,1)S(1)} %collective-permute-done.refs_1_), channel_id=1, source_target_pairs={{0,4},{1,5},{2,6},{3,7},{4,0},{5,1},{6,2},{7,3},{8,12},{9,13},{10,... | collective-permute-start | bytes 1671176 | tf_op jit(solution)/shard_map/ppermute | solution.py:339
  28.8 1.9 %collective-permute-start.11 = (bf16[128,2048]{1,0:T(8,128)(2,1)S(1)}, bf16[128,2048]{1,0:T(8,128)(2,1)S(1)}, u32[]{:S(2)}, u32[]{:S(2)}) collective-permute-start(bf16[128,2048]{1,0:T(8,128)(2,1)S(1)} %collective-permute-done.6.refs_8_), channel_id=1, source_target_pairs={{0,1},{1,0},{2,3},{3,2},{4,5},{5,4},{6,7},{7,6},{8,9},{9,8},{10,11... | collective-permute-start | bytes 1572872 | tf_op jit(solution)/shard_map/ppermute | solution.py:339
  28.8 14.3 %collective-permute-start.7 = (bf16[128,2048]{1,0:T(8,128)(2,1)S(1)}, bf16[128,2048]{1,0:T(8,128)(2,1)S(1)}, u32[]{:S(2)}, u32[]{:S(2)}) collective-permute-start(bf16[128,2048]{1,0:T(8,128)(2,1)S(1)} %collective-permute-done.6.refs_8_), channel_id=1, source_target_pairs={{0,2},{1,3},{2,0},{3,1},{4,6},{5,7},{6,4},{7,5},{8,10},{9,11},{10,... | collective-permute-start | bytes 1572872 | tf_op jit(solution)/shard_map/ppermute | solution.py:339
  43.2 2.7 %collective-permute-start.12 = (bf16[128,2176]{1,0:T(8,128)(2,1)S(1)}, bf16[128,2176]{1,0:T(8,128)(2,1)S(1)}, u32[]{:S(2)}, u32[]{:S(2)}) collective-permute-start(bf16[128,2176]{1,0:T(8,128)(2,1)S(1)} %collective-permute-done.5.refs_0_.refs_6_.refs_3_), channel_id=1, source_target_pairs={{0,1},{1,0},{2,3},{3,2},{4,5},{5,4},{6,7},{7,6},{8,9},{9,8},{10,11... | collective-permute-start | bytes 1671176 | tf_op jit(solution)/shard_map/ppermute | solution.py:339
  43.2 2.7 %collective-permute-start.13 = (bf16[128,2048]{1,0:T(8,128)(2,1)S(1)}, bf16[128,2048]{1,0:T(8,128)(2,1)S(1)}, u32[]{:S(2)}, u32[]{:S(2)}) collective-permute-start(bf16[128,2048]{1,0:T(8,128)(2,1)S(1)} %collective-permute-done.7.refs_1_), channel_id=1, source_target_pairs={{0,1},{1,0},{2,3},{3,2},{4,5},{5,4},{6,7},{7,6},{8,9},{9,8},{10,11... | collective-permute-start | bytes 1572872 | tf_op jit(solution)/shard_map/ppermute | solution.py:339
  47.9 28.1 %collective-permute-start.14 = (bf16[512,768]{1,0:T(8,128)(2,1)S(1)}, bf16[512,768]{1,0:T(8,128)(2,1)S(1)}, u32[]{:S(2)}, u32[]{:S(2)}) collective-permute-start(bf16[512,768]{1,0:T(8,128)(2,1)S(1)} %shard_map.125), channel_id=1, source_target_pairs={{0,8},{8,0},{16,24},{24,16},{1,9},{9,1},{17,25},{25,17},{2,10},{10... | collective-permute-start | bytes 2359304 | tf_op jit(solution)/shard_map/ppermute | solution.py:364
  50.8 25.1 %collective-permute-start.15 = (bf16[96,2048]{1,0:T(8,128)(2,1)S(1)}, bf16[96,2048]{1,0:T(8,128)(2,1)S(1)}, u32[]{:S(2)}, u32[]{:S(2)}) collective-permute-start(bf16[96,2048]{1,0:T(8,128)(2,1)S(1)} %get-tuple-element.83), channel_id=1, source_target_pairs={{0,8},{8,0},{16,24},{24,16},{1,9},{9,1},{17,25},{25,17},{2,10},{10... | collective-permute-start | bytes 1179656 | tf_op jit(solution)/shard_map/ppermute | solution.py:364
  76.6 4.2 %collective-permute-start.17 = (bf16[512,2048]{1,0:T(8,128)(2,1)S(1)}, bf16[512,2048]{1,0:T(8,128)(2,1)S(1)}, u32[]{:S(2)}, u32[]{:S(2)}) collective-permute-start(bf16[512,2048]{1,0:T(8,128)(2,1)S(1)} %get-tuple-element.96), channel_id=1, source_target_pairs={{0,1},{1,0},{2,3},{3,2},{4,5},{5,4},{6,7},{7,6},{8,9},{9,8},{10,11... | collective-permute-start | bytes 6291464 | tf_op jit(solution)/shard_map/ppermute | solution.py:339
  76.7 7.1 %collective-permute-start.18 = (bf16[512,2048]{1,0:T(8,128)(2,1)S(1)}, bf16[512,2048]{1,0:T(8,128)(2,1)S(1)}, u32[]{:S(2)}, u32[]{:S(2)}) collective-permute-start(bf16[512,2048]{1,0:T(8,128)(2,1)S(1)} %get-tuple-element.97), channel_id=1, source_target_pairs={{0,1},{1,0},{2,3},{3,2},{4,5},{5,4},{6,7},{7,6},{8,9},{9,8},{10,11... | collective-permute-start | bytes 6291464 | tf_op jit(solution)/shard_map/ppermute | solution.py:339
  77.2 28.8 %collective-permute-start.16 = (bf16[2304,256]{1,0:T(8,128)(2,1)S(1)}, bf16[2304,256]{1,0:T(8,128)(2,1)S(1)}, u32[]{:S(2)}, u32[]{:S(2)}) collective-permute-start(bf16[2304,256]{1,0:T(8,128)(2,1)S(1)} %shard_map.129), channel_id=1, source_target_pairs={{0,8},{8,24},{24,16},{16,0},{1,9},{9,25},{25,17},{17,1},{2,10},{10... | collective-permute-start | bytes 3538952 | tf_op jit(solution)/shard_map/ppermute | solution.py:364
  86.9 25.3 %collective-permute-start.19 = (bf16[256,2048]{1,0:T(8,128)(2,1)S(1)}, bf16[256,2048]{1,0:T(8,128)(2,1)S(1)}, u32[]{:S(2)}, u32[]{:S(2)}) collective-permute-start(bf16[256,2048]{1,0:T(8,128)(2,1)S(1)} %get-tuple-element.100), channel_id=1, source_target_pairs={{0,2},{1,3},{2,0},{3,1},{4,6},{5,7},{6,4},{7,5},{8,10},{9,11},{10,... | collective-permute-start | bytes 3145736 | tf_op jit(solution)/shard_map/ppermute | solution.py:339
  88.4 24.9 %collective-permute-start.20 = (bf16[256,2048]{1,0:T(8,128)(2,1)S(1)}, bf16[256,2048]{1,0:T(8,128)(2,1)S(1)}, u32[]{:S(2)}, u32[]{:S(2)}) collective-permute-start(bf16[256,2048]{1,0:T(8,128)(2,1)S(1)} %get-tuple-element.103), channel_id=1, source_target_pairs={{0,4},{1,5},{2,6},{3,7},{4,0},{5,1},{6,2},{7,3},{8,12},{9,13},{10,... | collective-permute-start | bytes 3145736 | tf_op jit(solution)/shard_map/ppermute | solution.py:339
  89.6 40.9 %collective-permute-start.24 = (bf16[2304,256]{1,0:T(8,128)(2,1)S(1)}, bf16[2304,256]{1,0:T(8,128)(2,1)S(1)}, u32[]{:S(2)}, u32[]{:S(2)}) collective-permute-start(bf16[2304,256]{1,0:T(8,128)(2,1)S(1)} %shard_map.131), channel_id=1, source_target_pairs={{0,8},{24,16},{1,9},{25,17},{2,10},{26,18},{3,11},{27,19},{4,12},{... | collective-permute-start | bytes 3538952 | tf_op jit(solution)/shard_map/ppermute | solution.py:364
  106.7 28.2 %collective-permute-start.23 = (bf16[2304,256]{1,0:T(8,128)(2,1)S(1)}, bf16[2304,256]{1,0:T(8,128)(2,1)S(1)}, u32[]{:S(2)}, u32[]{:S(2)}) collective-permute-start(bf16[2304,256]{1,0:T(8,128)(2,1)S(1)} %shard_map.132), channel_id=1, source_target_pairs={{8,16},{16,8},{9,17},{17,9},{10,18},{18,10},{11,19},{19,11},{12,20... | collective-permute-start | bytes 3538952 | tf_op jit(solution)/shard_map/ppermute | solution.py:364
  113.6 12.9 %collective-permute-start.21 = (bf16[128,2048]{1,0:T(8,128)(2,1)S(1)}, bf16[128,2048]{1,0:T(8,128)(2,1)S(1)}, u32[]{:S(2)}, u32[]{:S(2)}) collective-permute-start(bf16[128,2048]{1,0:T(8,128)(2,1)S(1)} %get-tuple-element.109), channel_id=1, source_target_pairs={{0,4},{1,5},{2,6},{3,7},{4,0},{5,1},{6,2},{7,3},{8,12},{9,13},{10,... | collective-permute-start | bytes 1572872 | tf_op jit(solution)/shard_map/ppermute | solution.py:339
  114.2 12.5 %collective-permute-start.22 = (bf16[128,2048]{1,0:T(8,128)(2,1)S(1)}, bf16[128,2048]{1,0:T(8,128)(2,1)S(1)}, u32[]{:S(2)}, u32[]{:S(2)}) collective-permute-start(bf16[128,2048]{1,0:T(8,128)(2,1)S(1)} %get-tuple-element.110), channel_id=1, source_target_pairs={{0,2},{1,3},{2,0},{3,1},{4,6},{5,7},{6,4},{7,5},{8,10},{9,11},{10,... | collective-permute-start | bytes 1572872 | tf_op jit(solution)/shard_map/ppermute | solution.py:339
